TPU v7x, 256 devices: a whole 4x4x8 slice. The times are simulated.
256 devices in a mesh: rep: 32 (over z_hi, y, x), node: 8 (over z_lo, core).
Axes of the slice: x: 4, y: 4, z: 8 (z_hi: 2, z_lo: 4; z = z_hi * 4 + z_lo), core: 2. Of those that a mesh axis runs over, the one named last changes fastest.
Arguments:
- attention: bfloat16 [65536, 2048], P(('rep', 'node')), may hold values from -6 to 6
- cotangent: bfloat16 [65536, 1792], P(('rep', 'node')), may hold values from -6 to 6
- token_ids: int32 [65536], P(('rep', 'node')), may hold values from 0 to 255999, as said below
- out_weight: bfloat16 [32, 2048, 1792], P('rep', 'node'), may hold values from -0.125 to 0.125
- moment: float32 [32, 2048, 1792], P('rep', 'node'), may hold values from -60 to 60
- second: float32 [32, 2048, 1792], P('rep', 'node'), may hold values from 100 to 4000
- norm_gain: float32 [32, 1792], P('rep'), may hold values from -0.5 to 0.5
- frag_index: int32 [1], replicated, may hold values from 0 to 7
- outer_delta: float32 [32, 8, 131072], P('rep', 'node'), may hold values from -6 to 6
- anchors: float32 [8, 131072], P(None, 'node'), may hold values from -6 to 6
- momenta: float32 [8, 131072], P(None, 'node'), may hold values from -3 to 3
- local_fragment: float32 [32, 131072], P('rep', 'node'), may hold values from -6 to 6
Outputs:
- new_weight: bfloat16 [32, 2048, 1792], P('rep', 'node')
- new_moment: float32 [32, 2048, 1792], P('rep', 'node')
- new_second: float32 [32, 2048, 1792], P('rep', 'node')
- grad_attention: bfloat16 [65536, 2048], P(('rep', 'node'))
- new_anchors: float32 [8, 131072], P(None, 'node')
- new_momenta: float32 [8, 131072], P(None, 'node')
- merged: float32 [32, 131072], P('rep')
Inputs may be any that keep to these rules, and one draw needn't show every extreme that they name: `token_ids`: 0 marks padding; every other entry is a vocabulary id.
All inputs are finite; a program needn't handle non-finite values.
Results may differ from a plain program's by a relative error of at most 0.015.
Values may be sent and summed in bfloat16 or wider, within the bound.
No kernel may reach another device: no remote copies, remote signals or barrier semaphores. Data moves between devices by JAX's collectives and lax.ppermute only.
A program may use at most 128 MiB of HBM per device.

v0:
```python
import jax
import jax.numpy as jnp
from jax import lax
from jax.sharding import PartitionSpec as P

beta_one = 0.9
beta_two = 0.95
adam_eps = 1e-08
inner_rate = 0.001
decay_rate = 0.1
inner_step = 10.0
outer_momentum = 0.9
outer_rate = 0.7
merge_weight = 0.5


def post_norm(values, gain):
    meansq = jnp.mean(values * values, axis=-1, keepdims=True)
    return values * lax.rsqrt(meansq + 1e-06) * (1.0 + gain)


def adamw(weight, moment, second, gradient):
    moment_new = beta_one * moment + (1.0 - beta_one) * gradient
    second_new = beta_two * second + (1.0 - beta_two) * gradient * gradient
    moment_hat = moment_new / (1.0 - beta_one**inner_step)
    second_hat = second_new / (1.0 - beta_two**inner_step)
    master = weight.astype(jnp.float32)
    updated = master - inner_rate * (
        moment_hat / (jnp.sqrt(second_hat) + adam_eps) + decay_rate * master
    )
    return (updated.astype(jnp.bfloat16), moment_new, second_new)


def nesterov(average, anchor, previous):
    momentum = outer_momentum * previous + average
    anchor_new = anchor - outer_rate * (average + outer_momentum * momentum)
    return (anchor_new, momentum)


def on_device(
    attention,
    cotangent,
    token_ids,
    out_weight,
    moment,
    second,
    norm_gain,
    frag_index,
    outer_delta,
    anchors,
    momenta,
    local_fragment,
):
    weight_shard = out_weight[0]
    gain = norm_gain[0]
    gathered = lax.all_gather(weight_shard, "node", axis=0, tiled=True)
    projected = jnp.dot(attention, gathered, preferred_element_type=jnp.float32)
    loss_mask = (token_ids != 0).astype(jnp.float32)
    weighted = cotangent.astype(jnp.float32) * loss_mask[:, None]
    _, pullback = jax.vjp(lambda values: post_norm(values, gain), projected)
    dprojected = pullback(weighted)[0].astype(jnp.bfloat16)
    grad_full = lax.dot_general(
        dprojected, gathered, (((1,), (1,)), ((), ())), preferred_element_type=jnp.float32
    )
    grad_attention = grad_full.astype(jnp.bfloat16)
    gradient = lax.psum_scatter(
        lax.dot_general(
            attention, dprojected, (((0,), (0,)), ((), ())), preferred_element_type=jnp.float32
        ).astype(jnp.bfloat16),
        "node",
        scatter_dimension=0,
        tiled=True,
    ).astype(jnp.float32)
    new_weight, new_moment, new_second = adamw(weight_shard, moment[0], second[0], gradient)
    index = frag_index[0]
    anchor = lax.dynamic_index_in_dim(anchors, index, 0, keepdims=False)
    previous = lax.dynamic_index_in_dim(momenta, index, 0, keepdims=False)
    node_summed = lax.psum_scatter(
        outer_delta[0, 0].astype(jnp.bfloat16), "node", scatter_dimension=0, tiled=True
    )
    replicas = lax.axis_size("rep")
    summed = lax.psum(node_summed, "rep").astype(jnp.float32)
    anchor_new, momentum = nesterov(summed / replicas, anchor, previous)
    new_anchors = lax.dynamic_update_index_in_dim(anchors, anchor_new, index, 0)
    new_momenta = lax.dynamic_update_index_in_dim(momenta, momentum, index, 0)
    merged_shard = merge_weight * local_fragment[0] + (1.0 - merge_weight) * anchor_new
    merged = lax.all_gather(merged_shard, "node", axis=0, tiled=True)
    return (
        new_weight[None],
        new_moment[None],
        new_second[None],
        grad_attention,
        new_anchors,
        new_momenta,
        merged[None],
    )


def solution(mesh):
    return jax.shard_map(
        on_device,
        mesh=mesh,
        in_specs=(
            P(("rep", "node"), None),
            P(("rep", "node"), None),
            P(("rep", "node")),
            P("rep", "node", None),
            P("rep", "node", None),
            P("rep", "node", None),
            P("rep", None),
            P(),
            P("rep", "node", None),
            P(None, "node"),
            P(None, "node"),
            P("rep", "node"),
        ),
        out_specs=(
            P("rep", "node", None),
            P("rep", "node", None),
            P("rep", "node", None),
            P(("rep", "node"), None),
            P(None, "node"),
            P(None, "node"),
            P("rep", None),
        ),
        check_vma=False,
    )
```

profile of v0, /device:TPU:1, one launch (start us, length us, event | category | flops | bytes accessed | tf_op | source)
XLA Modules:
  0.0 444.1 jit_solution(3556861425870457639)
XLA Ops:
  7.3 1.2 copy.38
  8.5 1.9 copy.39
  10.4 2.1 convert_reduce_fusion
  12.7 83.5 %all-gather.3.cloned.1.call-done = bf16[1,2048,1792]{2,1,0:T(8,128)(2,1)} async-done(((bf16[1,256,1792]{2,1,0:T(8,128)(2,1)}), bf16[1,2048,1792]{2,1,0:T(8,128)(2,1)}) %all-gather.3.cloned.1.call-update) | async-done | bytes 7340048 | tf_op jit(solution)/shard_map/all_gather | solution.py:56
  96.2 5.3 %multiply_reduce_fusion.1 = (f32[256]{0:T(256)S(1)}, f32[256]{0:T(256)S(1)}, f32[256,1792]{1,0:T(8,128)S(1)}) fusion(f32[1792]{0:T(1024)S(1)} %add_reduce_fusion, f32[256]{0:T(256)S(1)} %compare_convert_fusion, bf16[256,1792]{1,0:T(8,128)(2,1)S(1)} %copy-done.4, bf16[256,2048]{1,0:T(8,128)(2,1)S(1)} %copy-done, ...), kind=kOutput, calls=%fused_computation.19 | convolution fusion | flops 1882258944 | bytes 11151360 | tf_op jit(solution)/shard_map/dot_general | solution.py:57
  101.5 1.2 copy-done.2
  102.7 5.5 %fusion.4 = bf16[2048,1792]{0,1:T(8,128)(2,1)} fusion(bf16[256,2048]{1,0:T(8,128)(2,1)S(1)} %copy-done, f32[256,1792]{1,0:T(8,128)S(1)} %get-tuple-element.31, bf16[256,1792]{1,0:T(8,128)(2,1)S(1)} %copy-done.4, f32[256]{0:T(256)S(1)} %get-tuple-element.30, f32[256]{0:T(256)S(1)} %get-tuple-element.29, f32[1792]{0:T(1024)S(1)} %add_reduce_fusion, ...), kind=kOutput, calls=%fused_computation.5 | convolution fusion | flops 1886388224 | bytes 11151360 | tf_op jit(solution)/shard_map/dot_general | solution.py:67
  108.2 1.1 copy-done.3
  109.3 1.3 copy.25
  111.3 1.8 copy.26
  113.1 2.7 copy.27
  117.1 1.8 dynamic-slice_multiply_fusion
  118.9 49.4 %all-reduce.3.cloned.1.call-done = bf16[131072]{0:T(1024)(128)(2,1)} async-done(((bf16[131072]{0:T(1024)(128)(2,1)}), bf16[131072]{0:T(1024)(128)(2,1)}) %all-reduce.3.cloned.1.call-update) | async-done | bytes 262160
  169.0 199.1 %psum.7 = bf16[16384]{0:T(1024)(128)(2,1)} all-reduce(bf16[16384]{0:T(1024)(128)(2,1)S(1)} %dynamic-slice.1), channel_id=1, replica_groups=mesh['rep'=32,'node'=8] {'rep'}, use_global_device_ids=true, to_apply=%region_4.5 | all-reduce | flops 16384 | bytes 65536 | tf_op jit(solution)/shard_map/psum | solution.py:82
  368.1 1.6 add_multiply_fusion
  369.6 1.9 dynamic_update_slice.8
  372.1 0.8 copy-done.5
  372.8 44.2 %all_gather.7 = f32[131072]{0:T(1024)S(1)} all-gather(f32[16384]{0:T(1024)S(1)} %get-tuple-element.23), channel_id=1, replica_groups=mesh['rep'=32,'node'=8] {'node'}, dimensions={0}, use_global_device_ids=true | all-gather | bytes 589824 | tf_op jit(solution)/shard_map/all_gather | solution.py:87
  417.0 7.1 %fusion.5 = bf16[256,2048]{1,0:T(8,128)(2,1)} fusion(bf16[1,2048,1792]{2,1,0:T(8,128)(2,1)} %all-gather.3.cloned.1.call-done, f32[256,1792]{1,0:T(8,128)} %copy-done.2, bf16[256,1792]{1,0:T(8,128)(2,1)} %param.13, f32[256]{0:T(256)} %copy-done.7, f32[256]{0:T(256)S(1)} %get-tuple-element.29, f32[1792]{0:T(1024)S(1)} %add_reduce_fusion, ...), kind=kOutput, calls=%fused_computation.8 | convolution fusion | flops 1883242496 | bytes 11151360 | tf_op jit(solution)/shard_map/dot_general | solution.py:62
  424.1 5.9 %fusion.15 = (f32[1,256,1792]{1,2,0:T(8,128)}, bf16[1,256,1792]{1,2,0:T(8,128)(2,1)}, f32[1,256,1792]{1,2,0:T(8,128)}) fusion(bf16[256,1792]{0,1:T(8,128)(2,1)} %reduce-scatter.2.cloned.1.call-done, f32[1,256,1792]{1,2,0:T(8,128)} %copy.27, f32[1,256,1792]{1,2,0:T(8,128)S(1)} %copy.26, bf16[1,256,1792]{1,2,0:T(8,128)(2,1)} %copy.25), kind=kLoop, calls=%fused_computation.22 | loop fusion | flops 8257536 | bytes 10092544 | tf_op jit(solution)/shard_map/broadcast_in_dim | solution.py:91
  430.0 2.7 copy.30
  432.7 2.3 copy.28
  435.1 1.7 copy.29
  436.7 0.8 copy.40
  (32 shorter events, 2.1 us)
Async XLA Ops:
  7.2 89.0 %copy-start = (bf16[256,2048]{1,0:T(8,128)(2,1)S(1)}, bf16[256,2048]{1,0:T(8,128)(2,1)}, u32[]{:S(2)}) copy-start(bf16[256,2048]{1,0:T(8,128)(2,1)} %param.12) | copy-start | bytes 3145732
  7.2 5.4 %copy-start.9 = (s32[256]{0:T(256)S(1)}, s32[256]{0:T(256)}, u32[]{:S(2)}) copy-start(s32[256]{0:T(256)} %param.14) | copy-start | bytes 3076
  7.2 89.0 %copy-start.4 = (bf16[256,1792]{1,0:T(8,128)(2,1)S(1)}, bf16[256,1792]{1,0:T(8,128)(2,1)}, u32[]{:S(2)}) copy-start(bf16[256,1792]{1,0:T(8,128)(2,1)} %param.13) | copy-start | bytes 2752516
  7.2 5.4 %copy-start.8 = (f32[1,1792]{1,0:T(1,128)S(1)}, f32[1,1792]{1,0:T(1,128)}, u32[]{:S(2)}) copy-start(f32[1,1792]{1,0:T(1,128)} %param.18) | copy-start | bytes 21508
  7.2 3.2 copy-start.6
  7.2 88.9 %all-gather.3.cloned.1.call-start = ((), (), s32[]{:S(2)}) async-start(), calls=%async_computation.2 | async-start | bytes 8257536 | tf_op jit(solution)/shard_map/all_gather | solution.py:56
  10.4 157.9 %all-reduce.3.cloned.1.call-start = ((), (), s32[]{:S(2)}) async-start(), calls=%async_computation.3 | async-start | bytes 524288
  12.5 411.6 %reduce-scatter.2.cloned.1.call-start = ((), (), s32[]{:S(2)}) async-start(), calls=%async_computation.1 | async-start | bytes 8257536 | tf_op jit(solution)/shard_map/reduce_scatter | solution.py:66
  101.4 1.2 copy-start.2
  101.5 6.7 %copy-start.7 = (f32[256]{0:T(256)}, f32[256]{0:T(256)S(1)}, u32[]{:S(2)}) copy-start(f32[256]{0:T(256)S(1)} %get-tuple-element.30) | copy-start | bytes 3076
  108.1 1.2 copy-start.3
  113.1 2.7 copy-start.10
  372.1 0.8 copy-start.5
  432.7 2.3 copy-start.1
Sparse Core Ops, SparseCore 0:
  10.5 85.6 all-gather.2
  99.3 68.8 all-reduce.2
  171.0 85.9 reduce-scatter.1
where the time goes:
time: 445 us; the launch traced here: 444 us
  blocking collectives  243 us (55%)
  waiting for transfers between devices  133 us (30%)
  local copies, waits for them, and re-layouts  23.4 us (5%)
  matrix products  17.8 us (4%)
  between operations  15.2 us (3%)
  other arithmetic  11.4 us (3%)
    psum x1, blocking collectives, on_device(): summed = lax.psum(node_summed, 'rep').astype(jnp.float32)  199 us
    all_gather x1, waiting for transfers between devices, on_device(): gathered = lax.all_gather(weight_shard, 'node', axis=0, tiled=True)  83.5 us
    unnamed x4, waiting for transfers between devices  49.4 us
    all_gather x1, blocking collectives, on_device(): merged = lax.all_gather(merged_shard, 'node', axis=0, tiled=True)  44.2 us
    unnamed x33, local copies, waits for them, and re-layouts  21 us
  transfers between devices with their start and end apart: 3, of which 2 were waited for; matrix products, arithmetic and copies ran while one was open for 7% of the time, Pallas kernels for 0%

commit v1 on v0

v1 whole, which is shorter than its diff:
```python
import jax
import jax.numpy as jnp
from jax import lax
from jax.sharding import PartitionSpec as P

beta_one = 0.9
beta_two = 0.95
adam_eps = 1e-08
inner_rate = 0.001
decay_rate = 0.1
inner_step = 10.0
outer_momentum = 0.9
outer_rate = 0.7
merge_weight = 0.5

NODES = 8
CHIPS = 4
HALVES = 2

def links(*pairs):
    return [(2 * a + core, 2 * b + core) for a, b in pairs for core in range(2)]


RING = links((0, 1), (1, 2), (2, 3), (3, 0))


def adamw(weight, moment, second, gradient):
    moment_new = beta_one * moment + (1.0 - beta_one) * gradient
    second_new = beta_two * second + (1.0 - beta_two) * gradient * gradient
    moment_hat = moment_new / (1.0 - beta_one**inner_step)
    second_hat = second_new / (1.0 - beta_two**inner_step)
    master = weight.astype(jnp.float32)
    updated = master - inner_rate * (
        moment_hat / (jnp.sqrt(second_hat) + adam_eps) + decay_rate * master
    )
    return (updated.astype(jnp.bfloat16), moment_new, second_new)


def nesterov(average, anchor, previous):
    momentum = outer_momentum * previous + average
    anchor_new = anchor - outer_rate * (average + outer_momentum * momentum)
    return (anchor_new, momentum)


def after(value, *others):
    return lax.optimization_barrier((value, *others))[0]


def swapped(value, axis, size, mask):
    return lax.ppermute(value, axis, [(a, a ^ mask) for a in range(size)])


def on_device(
    attention,
    cotangent,
    token_ids,
    out_weight,
    moment,
    second,
    norm_gain,
    frag_index,
    outer_delta,
    anchors,
    momenta,
    local_fragment,
):
    node = lax.axis_index("node")
    replicas = lax.axis_size("rep")
    chip, core = node // 2, node % 2
    weight_shard = out_weight[0]
    second_moment = second[0]
    gain = 1.0 + norm_gain[0]
    rows, width = weight_shard.shape
    tokens, features = attention.shape
    span = width // HALVES
    f32 = jnp.float32
    part = rows // HALVES

    def send(value, pairs):
        return lax.ppermute(value, "node", pairs)

    def cross(value):
        return swapped(value, "node", NODES, 1)

    def columns(owner):
        return lax.dynamic_slice(attention, (0, owner * rows), (tokens, rows))

    turns = [(chip - step) % CHIPS for step in range(1, CHIPS + 1)]
    own_cols = [columns(c * 2 + core) for c in turns]
    twin_cols = [columns(c * 2 + 1 - core) for c in turns]
    own_t = [jnp.transpose(block) for block in own_cols]
    lent = cross(jnp.concatenate(twin_cols, axis=1))

    delta = outer_delta.reshape(-1)
    shard = delta.shape[0] // NODES

    def take(owner):
        return lax.dynamic_slice(delta, (owner * shard,), (shard,))

    give = [take((chip ^ m) * 2 + 1 - core).astype(jnp.bfloat16) for m in range(CHIPS)]
    got = swapped(jnp.concatenate(give), "node", NODES, 1)
    held = [
        take((chip ^ m) * 2 + core) + got[m * shard : (m + 1) * shard].astype(f32)
        for m in range(CHIPS)
    ]

    def product(total, left, right):
        return total + jnp.dot(left, right, preferred_element_type=f32)

    halves = [weight_shard[h * part : (h + 1) * part] for h in range(HALVES)]
    own_twin = cross(weight_shard)
    lent, own_twin, *held = lax.optimization_barrier((lent, own_twin, *held))
    away = [
        swapped(held[m].astype(jnp.bfloat16), "node", NODES, 2 * m) for m in range(1, CHIPS)
    ]
    projected = product(jnp.zeros((tokens, width), f32), own_cols[3], weight_shard)
    projected = product(projected, twin_cols[3], own_twin)

    one, two = send(halves[0], RING), send(after(halves[1], got), RING)
    one_twin = cross(one)
    two, projected, *away = lax.optimization_barrier((two, projected, *away))
    two_twin = cross(two)
    total = (held[0] + away[0].astype(f32)) + (away[1].astype(f32) + away[2].astype(f32))
    total = after(total, two_twin)
    other = swapped(total, "rep", replicas, 1)
    pairs = [jnp.concatenate([one, two, one_twin, two_twin])]
    both_cols = [jnp.concatenate(pair, axis=1) for pair in zip(own_cols, twin_cols)]

    one, two = send(one, RING), send(two, RING)
    one, other = lax.optimization_barrier((one, other))
    one_twin = cross(one)
    total = after(total + other, one_twin)
    other = swapped(total, "rep", replicas, 2)
    projected = product(projected, both_cols[0], pairs[0])
    two, other, projected = lax.optimization_barrier((two, other, projected))
    two_twin = cross(two)
    total = after(total + other, two_twin)
    other = swapped(total, "rep", replicas, 4)
    pairs.append(jnp.concatenate([one, two, one_twin, two_twin]))

    one, two = send(one, RING), send(two, RING)
    one, other = lax.optimization_barrier((one, other))
    one_twin = cross(one)
    total = after(total + other, one_twin)
    other = swapped(total, "rep", replicas, 8)
    projected = product(projected, both_cols[1], pairs[1])
    projected = product(projected, own_cols[2][:, :part], one)
    projected = product(projected, twin_cols[2][:, :part], one_twin)
    two, other, projected = lax.optimization_barrier((two, other, projected))
    two_twin = cross(two)
    total = total + other
    projected = product(projected, own_cols[2][:, part:], two)
    projected = product(projected, twin_cols[2][:, part:], two_twin)
    pairs.append(jnp.concatenate([one, two, one_twin, two_twin]))
    pairs.append(jnp.concatenate([weight_shard, own_twin]))
    rounded = after(total, two).astype(jnp.bfloat16)
    other = swapped(rounded, "rep", replicas, 16)

    loss_mask = (token_ids != 0).astype(f32)
    meansq = jnp.mean(projected * projected, axis=-1, keepdims=True)
    scale = lax.rsqrt(meansq + 1e-06)
    weighted = cotangent.astype(f32) * loss_mask[:, None] * gain
    inner = jnp.mean(weighted * projected, axis=-1, keepdims=True)
    curve = scale * scale * scale * inner
    ranges = [slice(h * span, (h + 1) * span) for h in range(HALVES)]
    pieces = [
        (scale * weighted[:, at] - curve * projected[:, at]).astype(jnp.bfloat16)
        for at in ranges
    ]

    dtwin = [cross(piece) for piece in pieces]
    lent_t = [jnp.transpose(lent[:, n * rows : (n + 1) * rows]) for n in range(CHIPS)]

    def partial(step, h, *event):
        mine = after(own_t[step], dtwin[h], *event)
        return jnp.dot(mine, pieces[h], preferred_element_type=f32) + jnp.dot(
            lent_t[step], dtwin[h], preferred_element_type=f32
        )

    both = range(HALVES)
    travelling, back = [], []
    for h in both:
        travelling.append(partial(0, h, *travelling).astype(jnp.bfloat16))
    opening = list(travelling)
    for step in range(1, CHIPS):
        arrived = [send(piece, RING) for piece in travelling]
        back.append(arrived)
        sums = []
        for h in both:
            event = [arrived[0]] if h == 0 else [travelling[0]]
            sums.append(partial(step, h, *event) + arrived[h].astype(f32))
            travelling[h] = sums[h].astype(jnp.bfloat16)
    gradient = jnp.concatenate(sums, axis=1)
    new_weight, new_moment, new_second = adamw(
        weight_shard, moment[0], second_moment, gradient
    )

    grad_attention = jnp.zeros((tokens, features), jnp.bfloat16)
    contract = (((1,), (1,)), ((), ()))
    dprojected = jnp.concatenate(pieces, axis=1)
    for which, owner in enumerate(turns):
        held_back = after(dprojected, back[1 + which // 2][0])
        block = lax.dot_general(
            held_back, pairs[which], contract, preferred_element_type=f32
        ).astype(jnp.bfloat16)
        for n, at in enumerate((core, 1 - core)):
            grad_attention = lax.dynamic_update_slice(
                grad_attention,
                block[:, n * rows : (n + 1) * rows],
                (0, (owner * 2 + at) * rows),
            )

    summed = rounded.astype(f32) + other.astype(f32)
    index = frag_index[0]
    anchor = lax.dynamic_index_in_dim(after(anchors, two), index, 0, keepdims=False)
    previous = lax.dynamic_index_in_dim(after(momenta, two), index, 0, keepdims=False)
    anchor_new, momentum = nesterov(summed / replicas, anchor, previous)
    due = jnp.arange(anchors.shape[0])[:, None] == index
    new_anchors = jnp.where(due, anchor_new[None], anchors)
    new_momenta = jnp.where(due, momentum[None], momenta)
    merged_shard = merge_weight * local_fragment[0] + (1.0 - merge_weight) * anchor_new
    sent = after(merged_shard.astype(jnp.bfloat16), *opening)
    parts = [swapped(sent, "node", NODES, 2 * m) for m in range(1, CHIPS)]
    parts = jnp.concatenate([sent, *after(parts, back[1][0])])
    other = cross(parts)
    merged = jnp.zeros((NODES * shard,), f32)
    for m in range(CHIPS):
        for block, at in ((parts, core), (other, 1 - core)):
            piece = block[m * shard : (m + 1) * shard].astype(f32)
            merged = lax.dynamic_update_slice(merged, piece, (((chip ^ m) * 2 + at) * shard,))
    return (
        new_weight[None],
        new_moment[None],
        new_second[None],
        grad_attention,
        new_anchors,
        new_momenta,
        merged.reshape(1, -1),
    )


def solution(mesh):
    return jax.shard_map(
        on_device,
        mesh=mesh,
        in_specs=(
            P(("rep", "node"), None),
            P(("rep", "node"), None),
            P(("rep", "node")),
            P("rep", "node", None),
            P("rep", "node", None),
            P("rep", "node", None),
            P("rep", None),
            P(),
            P("rep", "node", None),
            P(None, "node"),
            P(None, "node"),
            P("rep", "node"),
        ),
        out_specs=(
            P("rep", "node", None),
            P("rep", "node", None),
            P("rep", "node", None),
            P(("rep", "node"), None),
            P(None, "node"),
            P(None, "node"),
            P("rep", None),
        ),
        check_vma=False,
    )
```

time: 445 us -> 165 us (0.37)
  blocking collectives: 243 us -> 0 us
  waiting for transfers between devices: 133 us -> 82.2 us
  starting transfers between devices: 0.12 us -> 42.9 us
  local copies, waits for them, and re-layouts: 23.4 us -> 9.24 us
  between operations: 15.2 us -> 2.19 us
    psum x1 -> x0, blocking collectives: 199 us -> none  [on_device(): summed = lax.psum(node_summed, 'rep').astype(jnp.float32)]
    all_gather x1 -> x0, waiting for transfers between devices: 83.5 us -> none  [on_device(): gathered = lax.all_gather(weight_shard, 'node', axis=0, tiled=True)]
    ppermute x0 -> x35, waiting for transfers between devices: none -> 82.2 us  [the longest x12 75.9 us: send(): return lax.ppermute(value, 'node', pairs)]
    unnamed x4 -> x0, waiting for transfers between devices: 49.4 us -> none
    all_gather x1 -> x0, blocking collectives: 44.2 us -> none  [on_device(): merged = lax.all_gather(merged_shard, 'node', axis=0, tiled=True)]
    ppermute x0 -> x35, starting transfers between devices: none -> 42.9 us  [the longest x23 39.7 us: swapped(): return lax.ppermute(value, axis, [(a, a ^ mask) for a in range(size)])]
    unnamed x33 -> x42, local copies, waits for them, and re-layouts: 21 us -> 2.19 us
    broadcast_in_dim x1 -> x0, other arithmetic: 5.89 us -> none  [on_device(): new_second[None]]
  transfers between devices with their start and end apart: 3 -> 35, of which waited for: 2 -> 21; matrix products, arithmetic and copies ran while one was open for 7% -> 17% of each run, Pallas kernels for 0% -> 0%
where the time goes in v1:
time: 165 us; the launch traced here: 164 us
  waiting for transfers between devices  82.2 us (50%)
  starting transfers between devices  42.9 us (26%)
  matrix products  18.9 us (11%)
  local copies, waits for them, and re-layouts  9.24 us (6%)
  other arithmetic  8.48 us (5%)
  between operations  2.19 us (1%)
    ppermute x12, waiting for transfers between devices, send(): return lax.ppermute(value, 'node', pairs)  75.9 us
    ppermute x23, starting transfers between devices, swapped(): return lax.ppermute(value, axis, [(a, a ^ mask) for a in range(size)])  39.7 us
    dot_general x8, matrix products, product(): return total + jnp.dot(left, right, preferred_element_type=f32)  9.71 us
    ppermute x23, waiting for transfers between devices, swapped(): return lax.ppermute(value, axis, [(a, a ^ mask) for a in range(size)])  6.39 us
    dot_general x4, matrix products, on_device(): lax.dot_general(held_back, pairs[which], contract, preferred_element_type...  3.85 us
  transfers between devices with their start and end apart: 35, of which 21 were waited for; matrix products, arithmetic and copies ran while one was open for 17% of the time, Pallas kernels for 0%

profile of v1, /device:TPU:1, one launch (start us, length us, event | category | flops | bytes accessed | tf_op | source)
XLA Modules:
  0.0 163.9 jit_solution(4403794918338373632)
XLA Ops:
  3.0 3.2 %collective-permute-start = (bf16[65536]{0:T(1024)(128)(2,1)}, bf16[65536]{0:T(1024)(128)(2,1)}, u32[]{:S(2)}, u32[]{:S(2)}) collective-permute-start(bf16[65536]{0:T(1024)(128)(2,1)} %pad_maximum_fusion.3), channel_id=1, source_target_pairs={{0,1},{1,0},{2,3},{3,2},{4,5},{5,4},{6,7},{7,6},{8,9},{9,8},{10,11... | collective-permute-start | bytes 393224 | tf_op jit(solution)/shard_map/ppermute | solution.py:50
  6.2 2.1 %dynamic-slice_bitcast_fusion = (bf16[256,256]{0,1:T(8,128)(2,1)}, bf16[256,256]{1,0:T(8,128)(2,1)S(1)}, bf16[256,256]{1,0:T(8,128)(2,1)S(1)}, bf16[256,256]{1,0...) fusion(bf16[256,2048]{1,0:T(8,128)(2,1)} %param.12, ...), kind=kLoop, calls=%fused_computation.85 | loop fusion | bytes 2097184 | tf_op jit(solution)/shard_map/transpose | solution.py:91
  18.6 7.0 %collective-permute-done.9 = bf16[128,1792]{1,0:T(8,128)(2,1)} collective-permute-done((bf16[128,1792]{1,0:T(8,128)(2,1)}, bf16[128,1792]{1,0:T(8,128)(2,1)}, u32[]{:S(2)}, u32[]{:S(2)}) %collective-permute-start.9) | collective-permute-done | bytes 458784 | tf_op jit(solution)/shard_map/ppermute | solution.py:80
  29.1 2.5 %collective-permute-start.6 = (bf16[16384]{0:T(1024)(128)(2,1)S(1)}, bf16[16384]{0:T(1024)(128)(2,1)S(1)}, u32[]{:S(2)}, u32[]{:S(2)}) collective-permute-start(bf16[16384]{0:T(1024)(128)(2,1)S(1)} %get-tuple-element.54), channel_id=1, source_target_pairs={{0,6},{1,7},{2,4},{3,5},{4,2},{5,3},{6,0},{7,1},{8,14},{9,15},{10,... | collective-permute-start | bytes 98312 | tf_op jit(solution)/shard_map/ppermute | solution.py:50
  33.2 2.2 %collective-permute-done.1 = bf16[128,1792]{1,0:T(8,128)(2,1)S(1)} collective-permute-done((bf16[128,1792]{1,0:T(8,128)(2,1)}, bf16[128,1792]{1,0:T(8,128)(2,1)S(1)}, u32[]{:S(2)}, u32[]{:S(2)}) %collective-permute-start.1) | collective-permute-done | bytes 458784 | tf_op jit(solution)/shard_map/ppermute | solution.py:80
  35.5 1.9 %collective-permute-done.4 = bf16[16384]{0:T(1024)(128)(2,1)S(1)} collective-permute-done((bf16[16384]{0:T(1024)(128)(2,1)S(1)}, bf16[16384]{0:T(1024)(128)(2,1)S(1)}, u32[]{:S(2)}, u32[]{:S(2)}) %collective-permute-start.4) | collective-permute-done | bytes 32800 | tf_op jit(solution)/shard_map/ppermute | solution.py:50
  40.4 7.9 %collective-permute-done.10 = bf16[128,1792]{1,0:T(8,128)(2,1)S(1)} collective-permute-done((bf16[128,1792]{1,0:T(8,128)(2,1)}, bf16[128,1792]{1,0:T(8,128)(2,1)S(1)}, u32[]{:S(2)}, u32[]{:S(2)}) %collective-permute-start.10) | collective-permute-done | bytes 458784 | tf_op jit(solution)/shard_map/ppermute | solution.py:80
  48.3 3.8 %collective-permute-start.12 = (bf16[128,1792]{1,0:T(8,128)(2,1)S(1)}, bf16[128,1792]{1,0:T(8,128)(2,1)S(1)}, u32[]{:S(2)}, u32[]{:S(2)}) collective-permute-start(bf16[128,1792]{1,0:T(8,128)(2,1)S(1)} %collective-permute-done.10), channel_id=1, source_target_pairs={{0,1},{1,0},{2,3},{3,2},{4,5},{5,4},{6,7},{7,6},{8,9},{9,8},{10,11... | collective-permute-start | bytes 1376264 | tf_op jit(solution)/shard_map/ppermute | solution.py:50
  53.6 1.9 %collective-permute-start.13 = (f32[16384]{0:T(1024)S(1)}, f32[16384]{0:T(1024)S(1)}, u32[]{:S(2)}, u32[]{:S(2)}) collective-permute-start(f32[16384]{0:T(1024)S(1)} %add.376), channel_id=1, source_target_pairs={{0,16},{8,24},{16,0},{24,8},{32,48},{40,56},{48,32},{56,40},{64,80... | collective-permute-start | bytes 196616 | tf_op jit(solution)/shard_map/ppermute | solution.py:50
  55.6 2.5 %collective-permute-done.7 = bf16[128,1792]{1,0:T(8,128)(2,1)S(1)} collective-permute-done((bf16[128,1792]{1,0:T(8,128)(2,1)S(1)}, bf16[128,1792]{1,0:T(8,128)(2,1)S(1)}, u32[]{:S(2)}, u32[]{:S(2)}) %collective-permute-start.7) | collective-permute-done | bytes 458784 | tf_op jit(solution)/shard_map/ppermute | solution.py:80
  58.3 1.9 %collective-permute-start.16 = (bf16[128,1792]{1,0:T(8,128)(2,1)S(1)}, bf16[128,1792]{1,0:T(8,128)(2,1)S(1)}, u32[]{:S(2)}, u32[]{:S(2)}) collective-permute-start(bf16[128,1792]{1,0:T(8,128)(2,1)S(1)} %collective-permute-done.7), channel_id=1, source_target_pairs={{0,1},{1,0},{2,3},{3,2},{4,5},{5,4},{6,7},{7,6},{8,9},{9,8},{10,11... | collective-permute-start | bytes 1376264 | tf_op jit(solution)/shard_map/ppermute | solution.py:50
  62.6 6.2 %collective-permute-done.17 = bf16[128,1792]{1,0:T(8,128)(2,1)S(1)} collective-permute-done((bf16[128,1792]{1,0:T(8,128)(2,1)S(1)}, bf16[128,1792]{1,0:T(8,128)(2,1)S(1)}, u32[]{:S(2)}, u32[]{:S(2)}) %collective-permute-start.17) | collective-permute-done | bytes 458784 | tf_op jit(solution)/shard_map/ppermute | solution.py:80
  68.8 2.6 %collective-permute-start.19 = (bf16[128,1792]{1,0:T(8,128)(2,1)S(1)}, bf16[128,1792]{1,0:T(8,128)(2,1)S(1)}, u32[]{:S(2)}, u32[]{:S(2)}) collective-permute-start(bf16[128,1792]{1,0:T(8,128)(2,1)S(1)} %collective-permute-done.17), channel_id=1, source_target_pairs={{0,1},{1,0},{2,3},{3,2},{4,5},{5,4},{6,7},{7,6},{8,9},{9,8},{10,11... | collective-permute-start | bytes 1376264 | tf_op jit(solution)/shard_map/ppermute | solution.py:50
  73.4 3.0 %collective-permute-start.20 = (f32[16384]{0:T(1024)S(1)}, f32[16384]{0:T(1024)S(1)}, u32[]{:S(2)}, u32[]{:S(2)}) collective-permute-start(f32[16384]{0:T(1024)S(1)} %add.381), channel_id=1, source_target_pairs={{0,64},{8,72},{16,80},{24,88},{32,96},{40,104},{48,112},{56,120},{... | collective-permute-start | bytes 196616 | tf_op jit(solution)/shard_map/ppermute | solution.py:50
  80.3 6.0 %collective-permute-start.30 = (bf16[16384]{0:T(1024)(128)(2,1)S(1)}, bf16[16384]{0:T(1024)(128)(2,1)S(1)}, u32[]{:S(2)}, u32[]{:S(2)}) collective-permute-start(bf16[16384]{0:T(1024)(128)(2,1)S(1)} %add.423), channel_id=1, source_target_pairs={{0,128},{8,136},{16,144},{24,152},{32,160},{40,168},{48,176},{56,1... | collective-permute-start | bytes 98312 | tf_op jit(solution)/shard_map/ppermute | solution.py:50
  95.0 3.4 %collective-permute-start.33 = (bf16[16384]{0:T(1024)(128)(2,1)S(1)}, bf16[16384]{0:T(1024)(128)(2,1)S(1)}, u32[]{:S(2)}, u32[]{:S(2)}) collective-permute-start(bf16[16384]{0:T(1024)(128)(2,1)S(1)} %get-tuple-element.89), channel_id=1, source_target_pairs={{0,6},{1,7},{2,4},{3,5},{4,2},{5,3},{6,0},{7,1},{8,14},{9,15},{10,... | collective-permute-start | bytes 98312 | tf_op jit(solution)/shard_map/ppermute | solution.py:50
  100.8 10.5 %collective-permute-done.23 = bf16[256,896]{1,0:T(8,128)(2,1)S(1)} collective-permute-done((bf16[256,896]{1,0:T(8,128)(2,1)S(1)}, bf16[256,896]{1,0:T(8,128)(2,1)S(1)}, u32[]{:S(2)}, u32[]{:S(2)}) %collective-permute-start.23) | collective-permute-done | bytes 458784 | tf_op jit(solution)/shard_map/ppermute | solution.py:80
  112.1 9.1 %collective-permute-done.27 = bf16[256,896]{1,0:T(8,128)(2,1)S(1)} collective-permute-done((bf16[256,896]{1,0:T(8,128)(2,1)S(1)}, bf16[256,896]{1,0:T(8,128)(2,1)S(1)}, u32[]{:S(2)}, u32[]{:S(2)}) %collective-permute-start.27) | collective-permute-done | bytes 458784 | tf_op jit(solution)/shard_map/ppermute | solution.py:80
  121.6 9.4 %collective-permute-done.24 = bf16[256,896]{1,0:T(8,128)(2,1)S(1)} collective-permute-done((bf16[256,896]{1,0:T(8,128)(2,1)S(1)}, bf16[256,896]{1,0:T(8,128)(2,1)S(1)}, u32[]{:S(2)}, u32[]{:S(2)}) %collective-permute-start.24) | collective-permute-done | bytes 458784 | tf_op jit(solution)/shard_map/ppermute | solution.py:80
  131.0 3.5 %collective-permute-start.34 = (bf16[65536]{0:T(1024)(128)(2,1)S(1)}, bf16[65536]{0:T(1024)(128)(2,1)S(1)}, u32[]{:S(2)}, u32[]{:S(2)}) collective-permute-start(bf16[65536]{0:T(1024)(128)(2,1)S(1)} %pad_maximum_fusion.4), channel_id=1, source_target_pairs={{0,1},{1,0},{2,3},{3,2},{4,5},{5,4},{6,7},{7,6},{8,9},{9,8},{10,11... | collective-permute-start | bytes 393224 | tf_op jit(solution)/shard_map/ppermute | solution.py:50
  136.3 4.5 %collective-permute-done.28 = bf16[256,896]{1,0:T(8,128)(2,1)S(1)} collective-permute-done((bf16[256,896]{1,0:T(8,128)(2,1)S(1)}, bf16[256,896]{1,0:T(8,128)(2,1)S(1)}, u32[]{:S(2)}, u32[]{:S(2)}) %collective-permute-start.28) | collective-permute-done | bytes 458784 | tf_op jit(solution)/shard_map/ppermute | solution.py:80
  141.7 9.0 %collective-permute-done.25 = bf16[256,896]{1,0:T(8,128)(2,1)S(1)} collective-permute-done((bf16[256,896]{1,0:T(8,128)(2,1)S(1)}, bf16[256,896]{1,0:T(8,128)(2,1)S(1)}, u32[]{:S(2)}, u32[]{:S(2)}) %collective-permute-start.25) | collective-permute-done | bytes 458784 | tf_op jit(solution)/shard_map/ppermute | solution.py:80
  153.8 6.7 %collective-permute-done.29 = bf16[256,896]{1,0:T(8,128)(2,1)S(1)} collective-permute-done((bf16[256,896]{1,0:T(8,128)(2,1)S(1)}, bf16[256,896]{1,0:T(8,128)(2,1)S(1)}, u32[]{:S(2)}, u32[]{:S(2)}) %collective-permute-start.29) | collective-permute-done | bytes 458784 | tf_op jit(solution)/shard_map/ppermute | solution.py:80
  160.8 3.1 %fusion.2 = (bf16[1,256,1792]{2,1,0:T(8,128)(2,1)}, f32[1,256,1792]{2,1,0:T(8,128)}, f32[1,256,1792]{2,1,0:T(8,128)}) fusion(bf16[1,256,1792]{2,1,0:T(8,128)(2,1)S(1)} %copy-done, f32[1,256,896]{2,1,0:T(8,128)S(1)} %fusion.19, f32[1,256,896]{2,1,0:T(8,128)S(1)} %fusion.21, f32[1,256,1792]{2,1,0:T(8,128)S(1)} %copy-done.1, f32[1,256,1792]{2,1,0:T(8,128)S(1)} %copy-done.2), kind=kLoop, calls=%fused_computation.6 | loop fusion | flops 8257536 | bytes 11010048 | tf_op jit(solution)/shard_map/convert_element_type | solution.py:36
  (166 shorter events, 47.8 us)
Async XLA Ops:
  3.0 12.2 %collective-permute-start = (bf16[65536]{0:T(1024)(128)(2,1)}, bf16[65536]{0:T(1024)(128)(2,1)}, u32[]{:S(2)}, u32[]{:S(2)}) collective-permute-start(bf16[65536]{0:T(1024)(128)(2,1)} %pad_maximum_fusion.3), channel_id=1, source_target_pairs={{0,1},{1,0},{2,3},{3,2},{4,5},{5,4},{6,7},{7,6},{8,9},{9,8},{10,11... | collective-permute-start | bytes 393224 | tf_op jit(solution)/shard_map/ppermute | solution.py:50
  9.9 18.1 %collective-permute-start.2 = (bf16[256,1024]{1,0:T(8,128)(2,1)}, bf16[256,1024]{1,0:T(8,128)(2,1)S(1)}, u32[]{:S(2)}, u32[]{:S(2)}) collective-permute-start(bf16[256,1024]{1,0:T(8,128)(2,1)} %pad_maximum_fusion.2), channel_id=1, source_target_pairs={{0,1},{1,0},{2,3},{3,2},{4,5},{5,4},{6,7},{7,6},{8,9},{9,8},{10,11... | collective-permute-start | bytes 1572872 | tf_op jit(solution)/shard_map/ppermute | solution.py:50
  9.9 18.1 %collective-permute-start.3 = (bf16[256,1792]{1,0:T(8,128)(2,1)S(1)}, bf16[256,1792]{1,0:T(8,128)(2,1)}, u32[]{:S(2)}, u32[]{:S(2)}) collective-permute-start(bf16[256,1792]{1,0:T(8,128)(2,1)S(1)} %bitcast.75), channel_id=1, source_target_pairs={{0,1},{1,0},{2,3},{3,2},{4,5},{5,4},{6,7},{7,6},{8,9},{9,8},{10,11... | collective-permute-start | bytes 2752520 | tf_op jit(solution)/shard_map/ppermute | solution.py:50
  11.4 14.3 %collective-permute-start.9 = (bf16[128,1792]{1,0:T(8,128)(2,1)}, bf16[128,1792]{1,0:T(8,128)(2,1)}, u32[]{:S(2)}, u32[]{:S(2)}) collective-permute-start(bf16[128,1792]{1,0:T(8,128)(2,1)} %get-tuple-element.115), channel_id=1, source_target_pairs={{0,2},{1,3},{2,4},{3,5},{4,6},{5,7},{6,0},{7,1},{8,10},{9,11},{10,... | collective-permute-start | bytes 1376264 | tf_op jit(solution)/shard_map/ppermute | solution.py:80
  15.2 20.3 %collective-permute-start.1 = (bf16[128,1792]{1,0:T(8,128)(2,1)}, bf16[128,1792]{1,0:T(8,128)(2,1)S(1)}, u32[]{:S(2)}, u32[]{:S(2)}) collective-permute-start(bf16[128,1792]{1,0:T(8,128)(2,1)} %get-tuple-element.50), channel_id=1, source_target_pairs={{0,2},{1,3},{2,4},{3,5},{4,6},{5,7},{6,0},{7,1},{8,10},{9,11},{10,... | collective-permute-start | bytes 1376264 | tf_op jit(solution)/shard_map/ppermute | solution.py:80
  26.7 13.7 %collective-permute-start.14 = (bf16[128,1792]{1,0:T(8,128)(2,1)}, bf16[128,1792]{1,0:T(8,128)(2,1)S(1)}, u32[]{:S(2)}, u32[]{:S(2)}) collective-permute-start(bf16[128,1792]{1,0:T(8,128)(2,1)} %collective-permute-done.9), channel_id=1, source_target_pairs={{0,1},{1,0},{2,3},{3,2},{4,5},{5,4},{6,7},{7,6},{8,9},{9,8},{10,11... | collective-permute-start | bytes 1376264 | tf_op jit(solution)/shard_map/ppermute | solution.py:50
  28.0 9.4 %collective-permute-start.4 = (bf16[16384]{0:T(1024)(128)(2,1)S(1)}, bf16[16384]{0:T(1024)(128)(2,1)S(1)}, u32[]{:S(2)}, u32[]{:S(2)}) collective-permute-start(bf16[16384]{0:T(1024)(128)(2,1)S(1)} %get-tuple-element.52), channel_id=1, source_target_pairs={{0,2},{1,3},{2,0},{3,1},{4,6},{5,7},{6,4},{7,5},{8,10},{9,11},{10,... | collective-permute-start | bytes 98312 | tf_op jit(solution)/shard_map/ppermute | solution.py:50
  28.0 9.4 %collective-permute-start.5 = (bf16[16384]{0:T(1024)(128)(2,1)S(1)}, bf16[16384]{0:T(1024)(128)(2,1)S(1)}, u32[]{:S(2)}, u32[]{:S(2)}) collective-permute-start(bf16[16384]{0:T(1024)(128)(2,1)S(1)} %get-tuple-element.53), channel_id=1, source_target_pairs={{0,4},{1,5},{2,6},{3,7},{4,0},{5,1},{6,2},{7,3},{8,12},{9,13},{10,... | collective-permute-start | bytes 98312 | tf_op jit(solution)/shard_map/ppermute | solution.py:50
  35.5 12.8 %collective-permute-start.10 = (bf16[128,1792]{1,0:T(8,128)(2,1)}, bf16[128,1792]{1,0:T(8,128)(2,1)S(1)}, u32[]{:S(2)}, u32[]{:S(2)}) collective-permute-start(bf16[128,1792]{1,0:T(8,128)(2,1)} %collective-permute-done.9), channel_id=1, source_target_pairs={{0,2},{1,3},{2,4},{3,5},{4,6},{5,7},{6,0},{7,1},{8,10},{9,11},{10,... | collective-permute-start | bytes 1376264 | tf_op jit(solution)/shard_map/ppermute | solution.py:80
  38.4 19.7 %collective-permute-start.7 = (bf16[128,1792]{1,0:T(8,128)(2,1)S(1)}, bf16[128,1792]{1,0:T(8,128)(2,1)S(1)}, u32[]{:S(2)}, u32[]{:S(2)}) collective-permute-start(bf16[128,1792]{1,0:T(8,128)(2,1)S(1)} %collective-permute-done.1), channel_id=1, source_target_pairs={{0,2},{1,3},{2,4},{3,5},{4,6},{5,7},{6,0},{7,1},{8,10},{9,11},{10,... | collective-permute-start | bytes 1376264 | tf_op jit(solution)/shard_map/ppermute | solution.py:80
  39.8 8.5 %collective-permute-start.11 = (f32[16384]{0:T(1024)S(1)}, f32[16384]{0:T(1024)S(1)}, u32[]{:S(2)}, u32[]{:S(2)}) collective-permute-start(f32[16384]{0:T(1024)S(1)} %add_add_fusion.2), channel_id=1, source_target_pairs={{0,8},{8,0},{16,24},{24,16},{32,40},{40,32},{48,56},{56,48},{64,72... | collective-permute-start | bytes 196616 | tf_op jit(solution)/shard_map/ppermute | solution.py:50
  55.5 13.3 %collective-permute-start.17 = (bf16[128,1792]{1,0:T(8,128)(2,1)S(1)}, bf16[128,1792]{1,0:T(8,128)(2,1)S(1)}, u32[]{:S(2)}, u32[]{:S(2)}) collective-permute-start(bf16[128,1792]{1,0:T(8,128)(2,1)S(1)} %collective-permute-done.10), channel_id=1, source_target_pairs={{0,2},{1,3},{2,4},{3,5},{4,6},{5,7},{6,0},{7,1},{8,10},{9,11},{10,... | collective-permute-start | bytes 1376264 | tf_op jit(solution)/shard_map/ppermute | solution.py:80
  60.2 18.4 %collective-permute-start.15 = (bf16[128,1792]{1,0:T(8,128)(2,1)S(1)}, bf16[128,1792]{1,0:T(8,128)(2,1)S(1)}, u32[]{:S(2)}, u32[]{:S(2)}) collective-permute-start(bf16[128,1792]{1,0:T(8,128)(2,1)S(1)} %collective-permute-done.7), channel_id=1, source_target_pairs={{0,2},{1,3},{2,4},{3,5},{4,6},{5,7},{6,0},{7,1},{8,10},{9,11},{10,... | collective-permute-start | bytes 1376264 | tf_op jit(solution)/shard_map/ppermute | solution.py:80
  78.7 9.8 %collective-permute-start.21 = (bf16[128,1792]{1,0:T(8,128)(2,1)S(1)}, bf16[128,1792]{1,0:T(8,128)(2,1)S(1)}, u32[]{:S(2)}, u32[]{:S(2)}) collective-permute-start(bf16[128,1792]{1,0:T(8,128)(2,1)S(1)} %collective-permute-done.15), channel_id=1, source_target_pairs={{0,1},{1,0},{2,3},{3,2},{4,5},{5,4},{6,7},{7,6},{8,9},{9,8},{10,11... | collective-permute-start | bytes 1376264 | tf_op jit(solution)/shard_map/ppermute | solution.py:50
  94.8 26.7 %collective-permute-start.31 = (bf16[16384]{0:T(1024)(128)(2,1)S(1)}, bf16[16384]{0:T(1024)(128)(2,1)S(1)}, u32[]{:S(2)}, u32[]{:S(2)}) collective-permute-start(bf16[16384]{0:T(1024)(128)(2,1)S(1)} %get-tuple-element.89), channel_id=1, source_target_pairs={{0,2},{1,3},{2,0},{3,1},{4,6},{5,7},{6,4},{7,5},{8,10},{9,11},{10,... | collective-permute-start | bytes 98312 | tf_op jit(solution)/shard_map/ppermute | solution.py:50
  94.9 26.6 %collective-permute-start.32 = (bf16[16384]{0:T(1024)(128)(2,1)S(1)}, bf16[16384]{0:T(1024)(128)(2,1)S(1)}, u32[]{:S(2)}, u32[]{:S(2)}) collective-permute-start(bf16[16384]{0:T(1024)(128)(2,1)S(1)} %get-tuple-element.89), channel_id=1, source_target_pairs={{0,4},{1,5},{2,6},{3,7},{4,0},{5,1},{6,2},{7,3},{8,12},{9,13},{10,... | collective-permute-start | bytes 98312 | tf_op jit(solution)/shard_map/ppermute | solution.py:50
  95.0 26.6 %collective-permute-start.33 = (bf16[16384]{0:T(1024)(128)(2,1)S(1)}, bf16[16384]{0:T(1024)(128)(2,1)S(1)}, u32[]{:S(2)}, u32[]{:S(2)}) collective-permute-start(bf16[16384]{0:T(1024)(128)(2,1)S(1)} %get-tuple-element.89), channel_id=1, source_target_pairs={{0,6},{1,7},{2,4},{3,5},{4,2},{5,3},{6,0},{7,1},{8,14},{9,15},{10,... | collective-permute-start | bytes 98312 | tf_op jit(solution)/shard_map/ppermute | solution.py:50
  98.5 12.8 %collective-permute-start.23 = (bf16[256,896]{1,0:T(8,128)(2,1)S(1)}, bf16[256,896]{1,0:T(8,128)(2,1)S(1)}, u32[]{:S(2)}, u32[]{:S(2)}) collective-permute-start(bf16[256,896]{1,0:T(8,128)(2,1)S(1)} %fusion.24), channel_id=1, source_target_pairs={{0,2},{1,3},{2,4},{3,5},{4,6},{5,7},{6,0},{7,1},{8,10},{9,11},{10,... | collective-permute-start | bytes 1376264 | tf_op jit(solution)/shard_map/ppermute | solution.py:80
  98.5 22.6 %collective-permute-start.27 = (bf16[256,896]{1,0:T(8,128)(2,1)S(1)}, bf16[256,896]{1,0:T(8,128)(2,1)S(1)}, u32[]{:S(2)}, u32[]{:S(2)}) collective-permute-start(bf16[256,896]{1,0:T(8,128)(2,1)S(1)} %fusion.29), channel_id=1, source_target_pairs={{0,2},{1,3},{2,4},{3,5},{4,6},{5,7},{6,0},{7,1},{8,10},{9,11},{10,... | collective-permute-start | bytes 1376264 | tf_op jit(solution)/shard_map/ppermute | solution.py:80
  111.6 19.3 %collective-permute-start.24 = (bf16[256,896]{1,0:T(8,128)(2,1)S(1)}, bf16[256,896]{1,0:T(8,128)(2,1)S(1)}, u32[]{:S(2)}, u32[]{:S(2)}) collective-permute-start(bf16[256,896]{1,0:T(8,128)(2,1)S(1)} %fusion.25), channel_id=1, source_target_pairs={{0,2},{1,3},{2,4},{3,5},{4,6},{5,7},{6,0},{7,1},{8,10},{9,11},{10,... | collective-permute-start | bytes 1376264 | tf_op jit(solution)/shard_map/ppermute | solution.py:80
  121.5 19.3 %collective-permute-start.28 = (bf16[256,896]{1,0:T(8,128)(2,1)S(1)}, bf16[256,896]{1,0:T(8,128)(2,1)S(1)}, u32[]{:S(2)}, u32[]{:S(2)}) collective-permute-start(bf16[256,896]{1,0:T(8,128)(2,1)S(1)} %fusion.28), channel_id=1, source_target_pairs={{0,2},{1,3},{2,4},{3,5},{4,6},{5,7},{6,0},{7,1},{8,10},{9,11},{10,... | collective-permute-start | bytes 1376264 | tf_op jit(solution)/shard_map/ppermute | solution.py:80
  131.0 10.4 %collective-permute-start.34 = (bf16[65536]{0:T(1024)(128)(2,1)S(1)}, bf16[65536]{0:T(1024)(128)(2,1)S(1)}, u32[]{:S(2)}, u32[]{:S(2)}) collective-permute-start(bf16[65536]{0:T(1024)(128)(2,1)S(1)} %pad_maximum_fusion.4), channel_id=1, source_target_pairs={{0,1},{1,0},{2,3},{3,2},{4,5},{5,4},{6,7},{7,6},{8,9},{9,8},{10,11... | collective-permute-start | bytes 393224 | tf_op jit(solution)/shard_map/ppermute | solution.py:50
  134.9 15.8 %collective-permute-start.25 = (bf16[256,896]{1,0:T(8,128)(2,1)S(1)}, bf16[256,896]{1,0:T(8,128)(2,1)S(1)}, u32[]{:S(2)}, u32[]{:S(2)}) collective-permute-start(bf16[256,896]{1,0:T(8,128)(2,1)S(1)} %fusion.26), channel_id=1, source_target_pairs={{0,2},{1,3},{2,4},{3,5},{4,6},{5,7},{6,0},{7,1},{8,10},{9,11},{10,... | collective-permute-start | bytes 1376264 | tf_op jit(solution)/shard_map/ppermute | solution.py:80
  141.1 19.3 %collective-permute-start.29 = (bf16[256,896]{1,0:T(8,128)(2,1)S(1)}, bf16[256,896]{1,0:T(8,128)(2,1)S(1)}, u32[]{:S(2)}, u32[]{:S(2)}) collective-permute-start(bf16[256,896]{1,0:T(8,128)(2,1)S(1)} %fusion.27), channel_id=1, source_target_pairs={{0,2},{1,3},{2,4},{3,5},{4,6},{5,7},{6,0},{7,1},{8,10},{9,11},{10,... | collective-permute-start | bytes 1376264 | tf_op jit(solution)/shard_map/ppermute | solution.py:80
  (29 other events, 212.4 us)

commit v2 on v1

--- a/solution.py
+++ b/solution.py
@@ -82,15 +82,6 @@
     def cross(value):
         return swapped(value, "node", NODES, 1)
 
-    def columns(owner):
-        return lax.dynamic_slice(attention, (0, owner * rows), (tokens, rows))
-
-    turns = [(chip - step) % CHIPS for step in range(1, CHIPS + 1)]
-    own_cols = [columns(c * 2 + core) for c in turns]
-    twin_cols = [columns(c * 2 + 1 - core) for c in turns]
-    own_t = [jnp.transpose(block) for block in own_cols]
-    lent = cross(jnp.concatenate(twin_cols, axis=1))
-
     delta = outer_delta.reshape(-1)
     shard = delta.shape[0] // NODES
 
@@ -108,54 +99,59 @@
         return total + jnp.dot(left, right, preferred_element_type=f32)
 
     halves = [weight_shard[h * part : (h + 1) * part] for h in range(HALVES)]
-    own_twin = cross(weight_shard)
-    lent, own_twin, *held = lax.optimization_barrier((lent, own_twin, *held))
     away = [
         swapped(held[m].astype(jnp.bfloat16), "node", NODES, 2 * m) for m in range(1, CHIPS)
     ]
+
+    one = send(halves[0], RING)
+    two = after(send(after(halves[1], got), RING), one)
+    one_twin = cross(one)
+    two, *away = lax.optimization_barrier((two, *away))
+    two_twin = cross(two)
+    attention = after(attention, two)
+
+    def columns(owner):
+        return lax.dynamic_slice(attention, (0, owner * rows), (tokens, rows))
+
+    turns = [(chip - step) % CHIPS for step in range(1, CHIPS + 1)]
+    own_cols = [columns(c * 2 + core) for c in turns]
+    twin_cols = [columns(c * 2 + 1 - core) for c in turns]
+    own_t = [jnp.transpose(block) for block in own_cols]
+    lent = cross(jnp.concatenate(twin_cols, axis=1))
+
+    total = (held[0] + away[0].astype(f32)) + (away[1].astype(f32) + away[2].astype(f32))
+    total = after(total, two_twin)
+    total = total + swapped(total, "rep", replicas, 1)
+    total = total + swapped(total, "rep", replicas, 2)
+    own_twin = cross(after(weight_shard, two))
     projected = product(jnp.zeros((tokens, width), f32), own_cols[3], weight_shard)
     projected = product(projected, twin_cols[3], own_twin)
-
-    one, two = send(halves[0], RING), send(after(halves[1], got), RING)
-    one_twin = cross(one)
-    two, projected, *away = lax.optimization_barrier((two, projected, *away))
-    two_twin = cross(two)
-    total = (held[0] + away[0].astype(f32)) + (away[1].astype(f32) + away[2].astype(f32))
-    total = after(total, two_twin)
-    other = swapped(total, "rep", replicas, 1)
     pairs = [jnp.concatenate([one, two, one_twin, two_twin])]
     both_cols = [jnp.concatenate(pair, axis=1) for pair in zip(own_cols, twin_cols)]
 
-    one, two = send(one, RING), send(two, RING)
-    one, other = lax.optimization_barrier((one, other))
+    one, two = after(send(one, RING), two), send(two, RING)
     one_twin = cross(one)
-    total = after(total + other, one_twin)
-    other = swapped(total, "rep", replicas, 2)
+    two, total, projected, lent = lax.optimization_barrier(
+        (after(two, one), total, projected, lent)
+    )
+    two_twin = cross(two)
+    total = after(total, two_twin)
+    total = total + swapped(total, "rep", replicas, 4)
+    total = total + swapped(total, "rep", replicas, 8)
     projected = product(projected, both_cols[0], pairs[0])
-    two, other, projected = lax.optimization_barrier((two, other, projected))
-    two_twin = cross(two)
-    total = after(total + other, two_twin)
-    other = swapped(total, "rep", replicas, 4)
     pairs.append(jnp.concatenate([one, two, one_twin, two_twin]))
 
-    one, two = send(one, RING), send(two, RING)
-    one, other = lax.optimization_barrier((one, other))
+    one, two = after(send(one, RING), two), send(two, RING)
     one_twin = cross(one)
-    total = after(total + other, one_twin)
-    other = swapped(total, "rep", replicas, 8)
     projected = product(projected, both_cols[1], pairs[1])
     projected = product(projected, own_cols[2][:, :part], one)
     projected = product(projected, twin_cols[2][:, :part], one_twin)
-    two, other, projected = lax.optimization_barrier((two, other, projected))
+    two, total, projected = lax.optimization_barrier((two, total, projected))
     two_twin = cross(two)
-    total = total + other
     projected = product(projected, own_cols[2][:, part:], two)
     projected = product(projected, twin_cols[2][:, part:], two_twin)
     pairs.append(jnp.concatenate([one, two, one_twin, two_twin]))
     pairs.append(jnp.concatenate([weight_shard, own_twin]))
-    rounded = after(total, two).astype(jnp.bfloat16)
-    other = swapped(rounded, "rep", replicas, 16)
-
     loss_mask = (token_ids != 0).astype(f32)
     meansq = jnp.mean(projected * projected, axis=-1, keepdims=True)
     scale = lax.rsqrt(meansq + 1e-06)
@@ -181,15 +177,16 @@
     travelling, back = [], []
     for h in both:
         travelling.append(partial(0, h, *travelling).astype(jnp.bfloat16))
-    opening = list(travelling)
+    sent = [list(travelling)]
     for step in range(1, CHIPS):
         arrived = [send(piece, RING) for piece in travelling]
         back.append(arrived)
         sums = []
         for h in both:
-            event = [arrived[0]] if h == 0 else [travelling[0]]
+            event = [arrived[h], travelling[1 - h]]
             sums.append(partial(step, h, *event) + arrived[h].astype(f32))
             travelling[h] = sums[h].astype(jnp.bfloat16)
+        sent.append(list(travelling))
     gradient = jnp.concatenate(sums, axis=1)
     new_weight, new_moment, new_second = adamw(
         weight_shard, moment[0], second_moment, gradient
@@ -199,7 +196,7 @@
     contract = (((1,), (1,)), ((), ()))
     dprojected = jnp.concatenate(pieces, axis=1)
     for which, owner in enumerate(turns):
-        held_back = after(dprojected, back[1 + which // 2][0])
+        held_back = after(dprojected, sent[1 + which // 2][1])
         block = lax.dot_general(
             held_back, pairs[which], contract, preferred_element_type=f32
         ).astype(jnp.bfloat16)
@@ -210,18 +207,20 @@
                 (0, (owner * 2 + at) * rows),
             )
 
+    rounded = after(total.astype(jnp.bfloat16), *sent[0])
+    other = after(swapped(rounded, "rep", replicas, 16), sent[1][1])
     summed = rounded.astype(f32) + other.astype(f32)
     index = frag_index[0]
-    anchor = lax.dynamic_index_in_dim(after(anchors, two), index, 0, keepdims=False)
-    previous = lax.dynamic_index_in_dim(after(momenta, two), index, 0, keepdims=False)
+    anchor = lax.dynamic_index_in_dim(after(anchors, *sent[0]), index, 0, keepdims=False)
+    previous = lax.dynamic_index_in_dim(after(momenta, *sent[0]), index, 0, keepdims=False)
     anchor_new, momentum = nesterov(summed / replicas, anchor, previous)
     due = jnp.arange(anchors.shape[0])[:, None] == index
     new_anchors = jnp.where(due, anchor_new[None], anchors)
     new_momenta = jnp.where(due, momentum[None], momenta)
     merged_shard = merge_weight * local_fragment[0] + (1.0 - merge_weight) * anchor_new
-    sent = after(merged_shard.astype(jnp.bfloat16), *opening)
-    parts = [swapped(sent, "node", NODES, 2 * m) for m in range(1, CHIPS)]
-    parts = jnp.concatenate([sent, *after(parts, back[1][0])])
+    parts = merged_shard.astype(jnp.bfloat16)
+    parts = jnp.concatenate([parts, after(swapped(parts, "node", NODES, 2), sent[2][1])])
+    parts = jnp.concatenate([parts, swapped(parts, "node", NODES, 4)])
     other = cross(parts)
     merged = jnp.zeros((NODES * shard,), f32)
     for m in range(CHIPS):

time: 165 us -> 161 us (0.976)
  waiting for transfers between devices: 82.2 us -> 87 us
  other arithmetic: 8.48 us -> 5.06 us
  starting transfers between devices: 42.9 us -> 39.6 us
  matrix products: 18.9 us -> 16.5 us
    ppermute x23 -> x22, waiting for transfers between devices: 6.39 us -> 31.1 us  [swapped(): return lax.ppermute(value, axis, [(a, a ^ mask) for a in range(size)])]
    ppermute x12, waiting for transfers between devices: 75.9 us -> 55.9 us  [send(): return lax.ppermute(value, 'node', pairs)]
    ppermute x23 -> x22, starting transfers between devices: 39.7 us -> 36.5 us  [swapped(): return lax.ppermute(value, axis, [(a, a ^ mask) for a in range(size)])]
    unnamed x42 -> x58, local copies, waits for them, and re-layouts: 2.19 us -> 4.98 us
    add x7 -> x4, other arithmetic: 2.06 us -> 0.04 us  [the longest x1 0.01 us: on_device(): total = total + swapped(total, 'rep', replicas, 4)]
  transfers between devices with their start and end apart: 35 -> 34, of which waited for: 21 -> 19; matrix products, arithmetic and copies ran while one was open for 17% -> 13% of each run, Pallas kernels for 0% -> 0%
where the time goes in v2:
time: 161 us
  waiting for transfers between devices  87 us (54%)
  starting transfers between devices  39.6 us (25%)
  matrix products  16.5 us (10%)
  local copies, waits for them, and re-layouts  9.99 us (6%)
  other arithmetic  5.06 us (3%)
  between operations  2.44 us (2%)
    ppermute x12, waiting for transfers between devices, send(): return lax.ppermute(value, 'node', pairs)  55.9 us
    ppermute x22, starting transfers between devices, swapped(): return lax.ppermute(value, axis, [(a, a ^ mask) for a in range(size)])  36.5 us
    ppermute x22, waiting for transfers between devices, swapped(): return lax.ppermute(value, axis, [(a, a ^ mask) for a in range(size)])  31.1 us
    dot_general x8, matrix products, product(): return total + jnp.dot(left, right, preferred_element_type=f32)  8.62 us
    unnamed x58, local copies, waits for them, and re-layouts  4.98 us
  transfers between devices with their start and end apart: 34, of which 19 were waited for; matrix products, arithmetic and copies ran while one was open for 13% of the time, Pallas kernels for 0%

profile of v2, /device:TPU:1, one launch (start us, length us, event | category | flops | bytes accessed | tf_op | source)
XLA Modules:
  0.0 160.5 jit_solution(10410934171743890189)
XLA Ops:
  2.4 3.3 %collective-permute-start = (bf16[65536]{0:T(1024)(128)(2,1)S(1)}, bf16[65536]{0:T(1024)(128)(2,1)S(1)}, u32[]{:S(2)}, u32[]{:S(2)}) collective-permute-start(bf16[65536]{0:T(1024)(128)(2,1)S(1)} %pad_maximum_fusion.3), channel_id=1, source_target_pairs={{0,1},{1,0},{2,3},{3,2},{4,5},{5,4},{6,7},{7,6},{8,9},{9,8},{10,11... | collective-permute-start | bytes 393224 | tf_op jit(solution)/shard_map/ppermute | solution.py:50
  8.9 1.7 %collective-permute-start.3 = (bf16[16384]{0:T(1024)(128)(2,1)S(1)}, bf16[16384]{0:T(1024)(128)(2,1)S(1)}, u32[]{:S(2)}, u32[]{:S(2)}) collective-permute-start(bf16[16384]{0:T(1024)(128)(2,1)S(1)} %get-tuple-element.113), channel_id=1, source_target_pairs={{0,2},{1,3},{2,0},{3,1},{4,6},{5,7},{6,4},{7,5},{8,10},{9,11},{10,... | collective-permute-start | bytes 98312 | tf_op jit(solution)/shard_map/ppermute | solution.py:50
  11.1 1.7 %collective-permute-start.5 = (bf16[16384]{0:T(1024)(128)(2,1)S(1)}, bf16[16384]{0:T(1024)(128)(2,1)S(1)}, u32[]{:S(2)}, u32[]{:S(2)}) collective-permute-start(bf16[16384]{0:T(1024)(128)(2,1)S(1)} %get-tuple-element.111), channel_id=1, source_target_pairs={{0,6},{1,7},{2,4},{3,5},{4,2},{5,3},{6,0},{7,1},{8,14},{9,15},{10,... | collective-permute-start | bytes 98312 | tf_op jit(solution)/shard_map/ppermute | solution.py:50
  12.8 8.4 %collective-permute-done.2 = bf16[128,1792]{1,0:T(8,128)(2,1)} collective-permute-done((bf16[128,1792]{1,0:T(8,128)(2,1)S(1)}, bf16[128,1792]{1,0:T(8,128)(2,1)}, u32[]{:S(2)}, u32[]{:S(2)}) %collective-permute-start.2) | collective-permute-done | bytes 458784 | tf_op jit(solution)/shard_map/ppermute | solution.py:80
  23.6 7.3 %collective-permute-done.1 = bf16[128,1792]{1,0:T(8,128)(2,1)S(1)} collective-permute-done((bf16[128,1792]{1,0:T(8,128)(2,1)S(1)}, bf16[128,1792]{1,0:T(8,128)(2,1)S(1)}, u32[]{:S(2)}, u32[]{:S(2)}) %collective-permute-start.1) | collective-permute-done | bytes 458784 | tf_op jit(solution)/shard_map/ppermute | solution.py:80
  30.9 1.8 %collective-permute-done.3 = bf16[16384]{0:T(1024)(128)(2,1)S(1)} collective-permute-done((bf16[16384]{0:T(1024)(128)(2,1)S(1)}, bf16[16384]{0:T(1024)(128)(2,1)S(1)}, u32[]{:S(2)}, u32[]{:S(2)}) %collective-permute-start.3) | collective-permute-done | bytes 32800 | tf_op jit(solution)/shard_map/ppermute | solution.py:50
  37.9 5.7 %collective-permute-done.7 = bf16[128,1792]{1,0:T(8,128)(2,1)S(1)} collective-permute-done((bf16[128,1792]{1,0:T(8,128)(2,1)}, bf16[128,1792]{1,0:T(8,128)(2,1)S(1)}, u32[]{:S(2)}, u32[]{:S(2)}) %collective-permute-start.7) | collective-permute-done | bytes 458784 | tf_op jit(solution)/shard_map/ppermute | solution.py:80
  43.7 3.9 %collective-permute-start.11 = (bf16[256,1792]{1,0:T(8,128)(2,1)S(1)}, bf16[256,1792]{1,0:T(8,128)(2,1)S(1)}, u32[]{:S(2)}, u32[]{:S(2)}) collective-permute-start(bf16[256,1792]{1,0:T(8,128)(2,1)S(1)} %bitcast.75), channel_id=1, source_target_pairs={{0,1},{1,0},{2,3},{3,2},{4,5},{5,4},{6,7},{7,6},{8,9},{9,8},{10,11... | collective-permute-start | bytes 2752520 | tf_op jit(solution)/shard_map/ppermute | solution.py:50
  48.3 3.3 %collective-permute-done.9 = f32[16384]{0:T(1024)S(1)} collective-permute-done((f32[16384]{0:T(1024)S(1)}, f32[16384]{0:T(1024)S(1)}, u32[]{:S(2)}, u32[]{:S(2)}) %collective-permute-start.9) | collective-permute-done | bytes 65568 | tf_op jit(solution)/shard_map/ppermute | solution.py:50
  51.6 2.0 %collective-permute-start.10 = (f32[16384]{0:T(1024)S(1)}, f32[16384]{0:T(1024)S(1)}, u32[]{:S(2)}, u32[]{:S(2)}) collective-permute-start(f32[16384]{0:T(1024)S(1)} %add.364), channel_id=1, source_target_pairs={{0,16},{8,24},{16,0},{24,8},{32,48},{40,56},{48,32},{56,40},{64,80... | collective-permute-start | bytes 196616 | tf_op jit(solution)/shard_map/ppermute | solution.py:50
  54.2 3.2 %collective-permute-start.18 = (bf16[128,1792]{1,0:T(8,128)(2,1)S(1)}, bf16[128,1792]{1,0:T(8,128)(2,1)S(1)}, u32[]{:S(2)}, u32[]{:S(2)}) collective-permute-start(bf16[128,1792]{1,0:T(8,128)(2,1)S(1)} %collective-permute-done.7), channel_id=1, source_target_pairs={{0,1},{1,0},{2,3},{3,2},{4,5},{5,4},{6,7},{7,6},{8,9},{9,8},{10,11... | collective-permute-start | bytes 1376264 | tf_op jit(solution)/shard_map/ppermute | solution.py:50
  59.2 4.2 %collective-permute-done.19 = bf16[128,1792]{1,0:T(8,128)(2,1)S(1)} collective-permute-done((bf16[128,1792]{1,0:T(8,128)(2,1)S(1)}, bf16[128,1792]{1,0:T(8,128)(2,1)S(1)}, u32[]{:S(2)}, u32[]{:S(2)}) %collective-permute-start.19) | collective-permute-done | bytes 458784 | tf_op jit(solution)/shard_map/ppermute | solution.py:80
  63.4 3.5 %collective-permute-start.20 = (bf16[128,1792]{1,0:T(8,128)(2,1)S(1)}, bf16[128,1792]{1,0:T(8,128)(2,1)S(1)}, u32[]{:S(2)}, u32[]{:S(2)}) collective-permute-start(bf16[128,1792]{1,0:T(8,128)(2,1)S(1)} %collective-permute-done.19), channel_id=1, source_target_pairs={{0,1},{1,0},{2,3},{3,2},{4,5},{5,4},{6,7},{7,6},{8,9},{9,8},{10,11... | collective-permute-start | bytes 1376264 | tf_op jit(solution)/shard_map/ppermute | solution.py:50
  71.9 2.6 %collective-permute-start.16 = (f32[16384]{0:T(1024)S(1)}, f32[16384]{0:T(1024)S(1)}, u32[]{:S(2)}, u32[]{:S(2)}) collective-permute-start(f32[16384]{0:T(1024)S(1)} %add.378), channel_id=1, source_target_pairs={{0,64},{8,72},{16,80},{24,88},{32,96},{40,104},{48,112},{56,120},{... | collective-permute-start | bytes 196616 | tf_op jit(solution)/shard_map/ppermute | solution.py:50
  76.7 2.1 %collective-permute-start.21 = (bf16[128,1792]{1,0:T(8,128)(2,1)S(1)}, bf16[128,1792]{1,0:T(8,128)(2,1)S(1)}, u32[]{:S(2)}, u32[]{:S(2)}) collective-permute-start(bf16[128,1792]{1,0:T(8,128)(2,1)S(1)} %collective-permute-done.13), channel_id=1, source_target_pairs={{0,1},{1,0},{2,3},{3,2},{4,5},{5,4},{6,7},{7,6},{8,9},{9,8},{10,11... | collective-permute-start | bytes 1376264 | tf_op jit(solution)/shard_map/ppermute | solution.py:50
  80.2 1.8 %multiply_reduce_fusion.1 = (f32[256]{0:T(256)S(1)}, f32[256]{0:T(256)S(1)}, f32[256,1792]{1,0:T(8,128)S(1)}, f32[256,1792]{1,0:T(8,128)S(1)}) fusion(f32[1792]{0:T(1024)S(1)} %add_reduce_fusion, f32[256]{0:T(256)S(1)} %compare_convert_fusion, bf16[256,1792]{1,0:T(8,128)(2,1)S(1)} %copy-done.8, bf16[128,1792]{1,0:T(8,128)(2,1)S(1)} %collective-permute-done.21, ...), kind=kOutput, calls=%fused_computation.24 | convolution fusion | flops 121568768 | bytes 8792068 | tf_op jit(solution)/shard_map/dot_general | solution.py:99
  86.1 5.5 %collective-permute-start.30 = (bf16[16384]{0:T(1024)(128)(2,1)S(1)}, bf16[16384]{0:T(1024)(128)(2,1)S(1)}, u32[]{:S(2)}, u32[]{:S(2)}) collective-permute-start(bf16[16384]{0:T(1024)(128)(2,1)S(1)} %add.379), channel_id=1, source_target_pairs={{0,128},{8,136},{16,144},{24,152},{32,160},{40,168},{48,176},{56,1... | collective-permute-start | bytes 98312 | tf_op jit(solution)/shard_map/ppermute | solution.py:50
  93.7 5.5 %collective-permute-done.23 = bf16[256,896]{1,0:T(8,128)(2,1)S(1)} collective-permute-done((bf16[256,896]{1,0:T(8,128)(2,1)S(1)}, bf16[256,896]{1,0:T(8,128)(2,1)S(1)}, u32[]{:S(2)}, u32[]{:S(2)}) %collective-permute-start.23) | collective-permute-done | bytes 458784 | tf_op jit(solution)/shard_map/ppermute | solution.py:80
  99.6 9.4 %collective-permute-done.26 = bf16[256,896]{1,0:T(8,128)(2,1)S(1)} collective-permute-done((bf16[256,896]{1,0:T(8,128)(2,1)S(1)}, bf16[256,896]{1,0:T(8,128)(2,1)S(1)}, u32[]{:S(2)}, u32[]{:S(2)}) %collective-permute-start.26) | collective-permute-done | bytes 458784 | tf_op jit(solution)/shard_map/ppermute | solution.py:80
  113.5 6.0 %collective-permute-done.25 = bf16[256,896]{1,0:T(8,128)(2,1)S(1)} collective-permute-done((bf16[256,896]{1,0:T(8,128)(2,1)S(1)}, bf16[256,896]{1,0:T(8,128)(2,1)S(1)}, u32[]{:S(2)}, u32[]{:S(2)}) %collective-permute-start.25) | collective-permute-done | bytes 458784 | tf_op jit(solution)/shard_map/ppermute | solution.py:80
  120.1 9.4 %collective-permute-done.28 = bf16[256,896]{1,0:T(8,128)(2,1)S(1)} collective-permute-done((bf16[256,896]{1,0:T(8,128)(2,1)S(1)}, bf16[256,896]{1,0:T(8,128)(2,1)S(1)}, u32[]{:S(2)}, u32[]{:S(2)}) %collective-permute-start.28) | collective-permute-done | bytes 458784 | tf_op jit(solution)/shard_map/ppermute | solution.py:80
  129.8 1.9 %collective-permute-done.31 = bf16[16384]{0:T(1024)(128)(2,1)S(1)} collective-permute-done((bf16[16384]{0:T(1024)(128)(2,1)S(1)}, bf16[16384]{0:T(1024)(128)(2,1)S(1)}, u32[]{:S(2)}, u32[]{:S(2)}) %collective-permute-start.31) | collective-permute-done | bytes 32800 | tf_op jit(solution)/shard_map/ppermute | solution.py:50
  133.7 19.6 %collective-permute-done.32 = bf16[32768]{0:T(1024)(128)(2,1)S(1)} collective-permute-done((bf16[32768]{0:T(1024)(128)(2,1)S(1)}, bf16[32768]{0:T(1024)(128)(2,1)S(1)}, u32[]{:S(2)}, u32[]{:S(2)}) %collective-permute-start.32) | collective-permute-done | bytes 65568 | tf_op jit(solution)/shard_map/ppermute | solution.py:50
  157.4 3.1 %fusion.2 = (bf16[1,256,1792]{2,1,0:T(8,128)(2,1)}, f32[1,256,1792]{2,1,0:T(8,128)}, f32[1,256,1792]{2,1,0:T(8,128)}) fusion(bf16[1,256,1792]{2,1,0:T(8,128)(2,1)S(1)} %copy-done, f32[1,256,896]{2,1,0:T(8,128)S(1)} %fusion.17, f32[1,256,896]{2,1,0:T(8,128)S(1)} %fusion.19, f32[1,256,1792]{2,1,0:T(8,128)S(1)} %copy-done.5, f32[1,256,1792]{2,1,0:T(8,128)S(1)} %copy-done.6), kind=kLoop, calls=%fused_computation.6 | loop fusion | flops 8257536 | bytes 11010048 | tf_op jit(solution)/shard_map/convert_element_type | solution.py:36
  (177 shorter events, 41.3 us)
Async XLA Ops:
  7.0 14.2 %collective-permute-start.2 = (bf16[128,1792]{1,0:T(8,128)(2,1)S(1)}, bf16[128,1792]{1,0:T(8,128)(2,1)}, u32[]{:S(2)}, u32[]{:S(2)}) collective-permute-start(bf16[128,1792]{1,0:T(8,128)(2,1)S(1)} %get-tuple-element.100), channel_id=1, source_target_pairs={{0,2},{1,3},{2,4},{3,5},{4,6},{5,7},{6,0},{7,1},{8,10},{9,11},{10,... | collective-permute-start | bytes 1376264 | tf_op jit(solution)/shard_map/ppermute | solution.py:80
  7.3 23.6 %collective-permute-start.1 = (bf16[128,1792]{1,0:T(8,128)(2,1)S(1)}, bf16[128,1792]{1,0:T(8,128)(2,1)S(1)}, u32[]{:S(2)}, u32[]{:S(2)}) collective-permute-start(bf16[128,1792]{1,0:T(8,128)(2,1)S(1)} %get-tuple-element.42), channel_id=1, source_target_pairs={{0,2},{1,3},{2,4},{3,5},{4,6},{5,7},{6,0},{7,1},{8,10},{9,11},{10,... | collective-permute-start | bytes 1376264 | tf_op jit(solution)/shard_map/ppermute | solution.py:80
  8.9 23.8 %collective-permute-start.3 = (bf16[16384]{0:T(1024)(128)(2,1)S(1)}, bf16[16384]{0:T(1024)(128)(2,1)S(1)}, u32[]{:S(2)}, u32[]{:S(2)}) collective-permute-start(bf16[16384]{0:T(1024)(128)(2,1)S(1)} %get-tuple-element.113), channel_id=1, source_target_pairs={{0,2},{1,3},{2,0},{3,1},{4,6},{5,7},{6,4},{7,5},{8,10},{9,11},{10,... | collective-permute-start | bytes 98312 | tf_op jit(solution)/shard_map/ppermute | solution.py:50
  10.6 22.1 %collective-permute-start.4 = (bf16[16384]{0:T(1024)(128)(2,1)S(1)}, bf16[16384]{0:T(1024)(128)(2,1)S(1)}, u32[]{:S(2)}, u32[]{:S(2)}) collective-permute-start(bf16[16384]{0:T(1024)(128)(2,1)S(1)} %get-tuple-element.112), channel_id=1, source_target_pairs={{0,4},{1,5},{2,6},{3,7},{4,0},{5,1},{6,2},{7,3},{8,12},{9,13},{10,... | collective-permute-start | bytes 98312 | tf_op jit(solution)/shard_map/ppermute | solution.py:50
  11.1 21.6 %collective-permute-start.5 = (bf16[16384]{0:T(1024)(128)(2,1)S(1)}, bf16[16384]{0:T(1024)(128)(2,1)S(1)}, u32[]{:S(2)}, u32[]{:S(2)}) collective-permute-start(bf16[16384]{0:T(1024)(128)(2,1)S(1)} %get-tuple-element.111), channel_id=1, source_target_pairs={{0,6},{1,7},{2,4},{3,5},{4,2},{5,3},{6,0},{7,1},{8,14},{9,15},{10,... | collective-permute-start | bytes 98312 | tf_op jit(solution)/shard_map/ppermute | solution.py:50
  22.2 25.4 %collective-permute-start.17 = (bf16[128,1792]{1,0:T(8,128)(2,1)}, bf16[128,1792]{1,0:T(8,128)(2,1)S(1)}, u32[]{:S(2)}, u32[]{:S(2)}) collective-permute-start(bf16[128,1792]{1,0:T(8,128)(2,1)} %collective-permute-done.2), channel_id=1, source_target_pairs={{0,1},{1,0},{2,3},{3,2},{4,5},{5,4},{6,7},{7,6},{8,9},{9,8},{10,11... | collective-permute-start | bytes 1376264 | tf_op jit(solution)/shard_map/ppermute | solution.py:50
  30.9 12.8 %collective-permute-start.7 = (bf16[128,1792]{1,0:T(8,128)(2,1)}, bf16[128,1792]{1,0:T(8,128)(2,1)S(1)}, u32[]{:S(2)}, u32[]{:S(2)}) collective-permute-start(bf16[128,1792]{1,0:T(8,128)(2,1)} %collective-permute-done.2), channel_id=1, source_target_pairs={{0,2},{1,3},{2,4},{3,5},{4,6},{5,7},{6,0},{7,1},{8,10},{9,11},{10,... | collective-permute-start | bytes 1376264 | tf_op jit(solution)/shard_map/ppermute | solution.py:80
  32.7 15.0 %collective-permute-start.8 = (bf16[128,1792]{1,0:T(8,128)(2,1)S(1)}, bf16[128,1792]{1,0:T(8,128)(2,1)S(1)}, u32[]{:S(2)}, u32[]{:S(2)}) collective-permute-start(bf16[128,1792]{1,0:T(8,128)(2,1)S(1)} %collective-permute-done.1), channel_id=1, source_target_pairs={{0,1},{1,0},{2,3},{3,2},{4,5},{5,4},{6,7},{7,6},{8,9},{9,8},{10,11... | collective-permute-start | bytes 1376264 | tf_op jit(solution)/shard_map/ppermute | solution.py:50
  33.8 20.4 %collective-permute-start.6 = (bf16[128,1792]{1,0:T(8,128)(2,1)S(1)}, bf16[128,1792]{1,0:T(8,128)(2,1)S(1)}, u32[]{:S(2)}, u32[]{:S(2)}) collective-permute-start(bf16[128,1792]{1,0:T(8,128)(2,1)S(1)} %collective-permute-done.1), channel_id=1, source_target_pairs={{0,2},{1,3},{2,4},{3,5},{4,6},{5,7},{6,0},{7,1},{8,10},{9,11},{10,... | collective-permute-start | bytes 1376264 | tf_op jit(solution)/shard_map/ppermute | solution.py:80
  36.2 22.2 %collective-permute-start.12 = (bf16[256,1024]{1,0:T(8,128)(2,1)S(1)}, bf16[256,1024]{1,0:T(8,128)(2,1)S(1)}, u32[]{:S(2)}, u32[]{:S(2)}) collective-permute-start(bf16[256,1024]{1,0:T(8,128)(2,1)S(1)} %pad_maximum_fusion.2), channel_id=1, source_target_pairs={{0,1},{1,0},{2,3},{3,2},{4,5},{5,4},{6,7},{7,6},{8,9},{9,8},{10,11... | collective-permute-start | bytes 1572872 | tf_op jit(solution)/shard_map/ppermute | solution.py:50
  43.7 13.7 %collective-permute-start.11 = (bf16[256,1792]{1,0:T(8,128)(2,1)S(1)}, bf16[256,1792]{1,0:T(8,128)(2,1)S(1)}, u32[]{:S(2)}, u32[]{:S(2)}) collective-permute-start(bf16[256,1792]{1,0:T(8,128)(2,1)S(1)} %bitcast.75), channel_id=1, source_target_pairs={{0,1},{1,0},{2,3},{3,2},{4,5},{5,4},{6,7},{7,6},{8,9},{9,8},{10,11... | collective-permute-start | bytes 2752520 | tf_op jit(solution)/shard_map/ppermute | solution.py:50
  47.6 15.7 %collective-permute-start.19 = (bf16[128,1792]{1,0:T(8,128)(2,1)S(1)}, bf16[128,1792]{1,0:T(8,128)(2,1)S(1)}, u32[]{:S(2)}, u32[]{:S(2)}) collective-permute-start(bf16[128,1792]{1,0:T(8,128)(2,1)S(1)} %collective-permute-done.7), channel_id=1, source_target_pairs={{0,2},{1,3},{2,4},{3,5},{4,6},{5,7},{6,0},{7,1},{8,10},{9,11},{10,... | collective-permute-start | bytes 1376264 | tf_op jit(solution)/shard_map/ppermute | solution.py:80
  54.2 12.6 %collective-permute-start.18 = (bf16[128,1792]{1,0:T(8,128)(2,1)S(1)}, bf16[128,1792]{1,0:T(8,128)(2,1)S(1)}, u32[]{:S(2)}, u32[]{:S(2)}) collective-permute-start(bf16[128,1792]{1,0:T(8,128)(2,1)S(1)} %collective-permute-done.7), channel_id=1, source_target_pairs={{0,1},{1,0},{2,3},{3,2},{4,5},{5,4},{6,7},{7,6},{8,9},{9,8},{10,11... | collective-permute-start | bytes 1376264 | tf_op jit(solution)/shard_map/ppermute | solution.py:50
  59.2 17.5 %collective-permute-start.13 = (bf16[128,1792]{1,0:T(8,128)(2,1)S(1)}, bf16[128,1792]{1,0:T(8,128)(2,1)S(1)}, u32[]{:S(2)}, u32[]{:S(2)}) collective-permute-start(bf16[128,1792]{1,0:T(8,128)(2,1)S(1)} %collective-permute-done.6), channel_id=1, source_target_pairs={{0,2},{1,3},{2,4},{3,5},{4,6},{5,7},{6,0},{7,1},{8,10},{9,11},{10,... | collective-permute-start | bytes 1376264 | tf_op jit(solution)/shard_map/ppermute | solution.py:80
  63.4 11.1 %collective-permute-start.20 = (bf16[128,1792]{1,0:T(8,128)(2,1)S(1)}, bf16[128,1792]{1,0:T(8,128)(2,1)S(1)}, u32[]{:S(2)}, u32[]{:S(2)}) collective-permute-start(bf16[128,1792]{1,0:T(8,128)(2,1)S(1)} %collective-permute-done.19), channel_id=1, source_target_pairs={{0,1},{1,0},{2,3},{3,2},{4,5},{5,4},{6,7},{7,6},{8,9},{9,8},{10,11... | collective-permute-start | bytes 1376264 | tf_op jit(solution)/shard_map/ppermute | solution.py:50
  84.9 14.3 %collective-permute-start.23 = (bf16[256,896]{1,0:T(8,128)(2,1)S(1)}, bf16[256,896]{1,0:T(8,128)(2,1)S(1)}, u32[]{:S(2)}, u32[]{:S(2)}) collective-permute-start(bf16[256,896]{1,0:T(8,128)(2,1)S(1)} %fusion.24), channel_id=1, source_target_pairs={{0,2},{1,3},{2,4},{3,5},{4,6},{5,7},{6,0},{7,1},{8,10},{9,11},{10,... | collective-permute-start | bytes 1376264 | tf_op jit(solution)/shard_map/ppermute | solution.py:80
  86.0 23.0 %collective-permute-start.26 = (bf16[256,896]{1,0:T(8,128)(2,1)S(1)}, bf16[256,896]{1,0:T(8,128)(2,1)S(1)}, u32[]{:S(2)}, u32[]{:S(2)}) collective-permute-start(bf16[256,896]{1,0:T(8,128)(2,1)S(1)} %fusion.25), channel_id=1, source_target_pairs={{0,2},{1,3},{2,4},{3,5},{4,6},{5,7},{6,0},{7,1},{8,10},{9,11},{10,... | collective-permute-start | bytes 1376264 | tf_op jit(solution)/shard_map/ppermute | solution.py:80
  86.1 25.6 %collective-permute-start.30 = (bf16[16384]{0:T(1024)(128)(2,1)S(1)}, bf16[16384]{0:T(1024)(128)(2,1)S(1)}, u32[]{:S(2)}, u32[]{:S(2)}) collective-permute-start(bf16[16384]{0:T(1024)(128)(2,1)S(1)} %add.379), channel_id=1, source_target_pairs={{0,128},{8,136},{16,144},{24,152},{32,160},{40,168},{48,176},{56,1... | collective-permute-start | bytes 98312 | tf_op jit(solution)/shard_map/ppermute | solution.py:50
  99.5 20.0 %collective-permute-start.25 = (bf16[256,896]{1,0:T(8,128)(2,1)S(1)}, bf16[256,896]{1,0:T(8,128)(2,1)S(1)}, u32[]{:S(2)}, u32[]{:S(2)}) collective-permute-start(bf16[256,896]{1,0:T(8,128)(2,1)S(1)} %fusion.26), channel_id=1, source_target_pairs={{0,2},{1,3},{2,4},{3,5},{4,6},{5,7},{6,0},{7,1},{8,10},{9,11},{10,... | collective-permute-start | bytes 1376264 | tf_op jit(solution)/shard_map/ppermute | solution.py:80
  109.4 20.0 %collective-permute-start.28 = (bf16[256,896]{1,0:T(8,128)(2,1)S(1)}, bf16[256,896]{1,0:T(8,128)(2,1)S(1)}, u32[]{:S(2)}, u32[]{:S(2)}) collective-permute-start(bf16[256,896]{1,0:T(8,128)(2,1)S(1)} %fusion.27), channel_id=1, source_target_pairs={{0,2},{1,3},{2,4},{3,5},{4,6},{5,7},{6,0},{7,1},{8,10},{9,11},{10,... | collective-permute-start | bytes 1376264 | tf_op jit(solution)/shard_map/ppermute | solution.py:80
  111.8 20.0 %collective-permute-start.31 = (bf16[16384]{0:T(1024)(128)(2,1)S(1)}, bf16[16384]{0:T(1024)(128)(2,1)S(1)}, u32[]{:S(2)}, u32[]{:S(2)}) collective-permute-start(bf16[16384]{0:T(1024)(128)(2,1)S(1)} %get-tuple-element.84), channel_id=1, source_target_pairs={{0,2},{1,3},{2,0},{3,1},{4,6},{5,7},{6,4},{7,5},{8,10},{9,11},{10,... | collective-permute-start | bytes 98312 | tf_op jit(solution)/shard_map/ppermute | solution.py:50
  120.0 35.1 %collective-permute-start.27 = (bf16[256,896]{1,0:T(8,128)(2,1)S(1)}, bf16[256,896]{1,0:T(8,128)(2,1)S(1)}, u32[]{:S(2)}, u32[]{:S(2)}) collective-permute-start(bf16[256,896]{1,0:T(8,128)(2,1)S(1)} %fusion.28), channel_id=1, source_target_pairs={{0,2},{1,3},{2,4},{3,5},{4,6},{5,7},{6,0},{7,1},{8,10},{9,11},{10,... | collective-permute-start | bytes 1376264 | tf_op jit(solution)/shard_map/ppermute | solution.py:80
  129.8 25.3 %collective-permute-start.29 = (bf16[256,896]{1,0:T(8,128)(2,1)S(1)}, bf16[256,896]{1,0:T(8,128)(2,1)S(1)}, u32[]{:S(2)}, u32[]{:S(2)}) collective-permute-start(bf16[256,896]{1,0:T(8,128)(2,1)S(1)} %fusion.29), channel_id=1, source_target_pairs={{0,2},{1,3},{2,4},{3,5},{4,6},{5,7},{6,0},{7,1},{8,10},{9,11},{10,... | collective-permute-start | bytes 1376264 | tf_op jit(solution)/shard_map/ppermute | solution.py:80
  131.7 21.6 %collective-permute-start.32 = (bf16[32768]{0:T(1024)(128)(2,1)S(1)}, bf16[32768]{0:T(1024)(128)(2,1)S(1)}, u32[]{:S(2)}, u32[]{:S(2)}) collective-permute-start(bf16[32768]{0:T(1024)(128)(2,1)S(1)} %pad_maximum_fusion.5), channel_id=1, source_target_pairs={{0,4},{1,5},{2,6},{3,7},{4,0},{5,1},{6,2},{7,3},{8,12},{9,13},{10,... | collective-permute-start | bytes 196616 | tf_op jit(solution)/shard_map/ppermute | solution.py:50
  (36 other events, 202.8 us)

commit v3 on v2

--- a/solution.py
+++ b/solution.py
@@ -82,7 +82,8 @@
     def cross(value):
         return swapped(value, "node", NODES, 1)
 
-    delta = outer_delta.reshape(-1)
+    halves = [weight_shard[h * part : (h + 1) * part] for h in range(HALVES)]
+    delta = after(outer_delta.reshape(-1), *halves)
     shard = delta.shape[0] // NODES
 
     def take(owner):
@@ -98,7 +99,6 @@
     def product(total, left, right):
         return total + jnp.dot(left, right, preferred_element_type=f32)
 
-    halves = [weight_shard[h * part : (h + 1) * part] for h in range(HALVES)]
     away = [
         swapped(held[m].astype(jnp.bfloat16), "node", NODES, 2 * m) for m in range(1, CHIPS)
     ]
@@ -120,7 +120,6 @@
     lent = cross(jnp.concatenate(twin_cols, axis=1))
 
     total = (held[0] + away[0].astype(f32)) + (away[1].astype(f32) + away[2].astype(f32))
-    total = after(total, two_twin)
     total = total + swapped(total, "rep", replicas, 1)
     total = total + swapped(total, "rep", replicas, 2)
     own_twin = cross(after(weight_shard, two))
@@ -130,18 +129,19 @@
     both_cols = [jnp.concatenate(pair, axis=1) for pair in zip(own_cols, twin_cols)]
 
     one, two = after(send(one, RING), two), send(two, RING)
+    one, total = lax.optimization_barrier((one, total))
     one_twin = cross(one)
-    two, total, projected, lent = lax.optimization_barrier(
-        (after(two, one), total, projected, lent)
-    )
-    two_twin = cross(two)
-    total = after(total, two_twin)
     total = total + swapped(total, "rep", replicas, 4)
     total = total + swapped(total, "rep", replicas, 8)
+    passed_two = after(two, one)
+    two, total, projected, lent = lax.optimization_barrier(
+        (passed_two, total, projected, lent)
+    )
+    two_twin = cross(two)
     projected = product(projected, both_cols[0], pairs[0])
     pairs.append(jnp.concatenate([one, two, one_twin, two_twin]))
 
-    one, two = after(send(one, RING), two), send(two, RING)
+    one, two = after(send(one, RING), two), send(passed_two, RING)
     one_twin = cross(one)
     projected = product(projected, both_cols[1], pairs[1])
     projected = product(projected, own_cols[2][:, :part], one)

time: 161 us -> 156 us (0.969)
  matrix products: 16.5 us -> 13.1 us
  waiting for transfers between devices: 87 us -> 89.8 us
  starting transfers between devices: 39.6 us -> 36.9 us
  local copies, waits for them, and re-layouts: 9.99 us -> 8.08 us
    ppermute x22, waiting for transfers between devices: 31.1 us -> 34.6 us  [swapped(): return lax.ppermute(value, axis, [(a, a ^ mask) for a in range(size)])]
    dot_general x8, matrix products: 8.62 us -> 5.18 us  [product(): return total + jnp.dot(left, right, preferred_element_type=f32)]
    ppermute x22, starting transfers between devices: 36.5 us -> 34.3 us  [swapped(): return lax.ppermute(value, axis, [(a, a ^ mask) for a in range(size)])]
    convert_element_type x1 -> x0, local copies, waits for them, and re-layouts: 1.68 us -> none  [on_device(): take((chip ^ m) * 2 + 1 - core).astype(jnp.bfloat16)]
    unnamed x58 -> x60, local copies, waits for them, and re-layouts: 4.98 us -> 5.86 us
  transfers between devices with their start and end apart: 34 -> 34, of which waited for: 19 -> 21; matrix products, arithmetic and copies ran while one was open for 13% -> 10% of each run, Pallas kernels for 0% -> 0%
where the time goes in v3:
time: 156 us; the launch traced here: 155 us
  waiting for transfers between devices  89.8 us (58%)
  starting transfers between devices  36.9 us (24%)
  matrix products  13.1 us (8%)
  local copies, waits for them, and re-layouts  8.08 us (5%)
  other arithmetic  5.05 us (3%)
  between operations  2.35 us (2%)
    ppermute x12, waiting for transfers between devices, send(): return lax.ppermute(value, 'node', pairs)  55.2 us
    ppermute x22, waiting for transfers between devices, swapped(): return lax.ppermute(value, axis, [(a, a ^ mask) for a in range(size)])  34.6 us
    ppermute x22, starting transfers between devices, swapped(): return lax.ppermute(value, axis, [(a, a ^ mask) for a in range(size)])  34.3 us
    unnamed x60, local copies, waits for them, and re-layouts  5.86 us
    dot_general x8, matrix products, product(): return total + jnp.dot(left, right, preferred_element_type=f32)  5.18 us
    convert_element_type x1, other arithmetic, adamw(): return (updated.astype(jnp.bfloat16), moment_new, second_new)  3.14 us
  transfers between devices with their start and end apart: 34, of which 21 were waited for; matrix products, arithmetic and copies ran while one was open for 10% of the time, Pallas kernels for 0%

profile of v3, /device:TPU:1, one launch (start us, length us, event | category | flops | bytes accessed | tf_op | source)
XLA Modules:
  0.0 155.4 jit_solution(12784112743594350712)
XLA Ops:
  2.1 3.3 %collective-permute-start = (bf16[65536]{0:T(1024)(128)(2,1)S(1)}, bf16[65536]{0:T(1024)(128)(2,1)S(1)}, u32[]{:S(2)}, u32[]{:S(2)}) collective-permute-start(bf16[65536]{0:T(1024)(128)(2,1)S(1)} %pad_maximum_fusion.3), channel_id=1, source_target_pairs={{0,1},{1,0},{2,3},{3,2},{4,5},{5,4},{6,7},{7,6},{8,9},{9,8},{10,11... | collective-permute-start | bytes 393224 | tf_op jit(solution)/shard_map/ppermute | solution.py:50
  7.3 1.7 %collective-permute-start.3 = (bf16[16384]{0:T(1024)(128)(2,1)S(1)}, bf16[16384]{0:T(1024)(128)(2,1)S(1)}, u32[]{:S(2)}, u32[]{:S(2)}) collective-permute-start(bf16[16384]{0:T(1024)(128)(2,1)S(1)} %get-tuple-element.102), channel_id=1, source_target_pairs={{0,2},{1,3},{2,0},{3,1},{4,6},{5,7},{6,4},{7,5},{8,10},{9,11},{10,... | collective-permute-start | bytes 98312 | tf_op jit(solution)/shard_map/ppermute | solution.py:50
  11.2 8.3 %collective-permute-done.2 = bf16[128,1792]{1,0:T(8,128)(2,1)} collective-permute-done((bf16[128,1792]{1,0:T(8,128)(2,1)S(1)}, bf16[128,1792]{1,0:T(8,128)(2,1)}, u32[]{:S(2)}, u32[]{:S(2)}) %collective-permute-start.2) | collective-permute-done | bytes 458784 | tf_op jit(solution)/shard_map/ppermute | solution.py:80
  22.1 7.1 %collective-permute-done.1 = bf16[128,1792]{1,0:T(8,128)(2,1)S(1)} collective-permute-done((bf16[128,1792]{1,0:T(8,128)(2,1)S(1)}, bf16[128,1792]{1,0:T(8,128)(2,1)S(1)}, u32[]{:S(2)}, u32[]{:S(2)}) %collective-permute-start.1) | collective-permute-done | bytes 458784 | tf_op jit(solution)/shard_map/ppermute | solution.py:80
  29.2 1.9 %collective-permute-done.3 = bf16[16384]{0:T(1024)(128)(2,1)S(1)} collective-permute-done((bf16[16384]{0:T(1024)(128)(2,1)S(1)}, bf16[16384]{0:T(1024)(128)(2,1)S(1)}, u32[]{:S(2)}, u32[]{:S(2)}) %collective-permute-start.3) | collective-permute-done | bytes 32800 | tf_op jit(solution)/shard_map/ppermute | solution.py:50
  36.7 2.2 %collective-permute-start.9 = (f32[16384]{0:T(1024)S(1)}, f32[16384]{0:T(1024)S(1)}, u32[]{:S(2)}, u32[]{:S(2)}) collective-permute-start(f32[16384]{0:T(1024)S(1)} %add.364), channel_id=1, source_target_pairs={{0,16},{8,24},{16,0},{24,8},{32,48},{40,56},{48,32},{56,40},{64,80... | collective-permute-start | bytes 196616 | tf_op jit(solution)/shard_map/ppermute | solution.py:50
  38.9 2.6 %collective-permute-done.9 = f32[16384]{0:T(1024)S(1)} collective-permute-done((f32[16384]{0:T(1024)S(1)}, f32[16384]{0:T(1024)S(1)}, u32[]{:S(2)}, u32[]{:S(2)}) %collective-permute-start.9) | collective-permute-done | bytes 65568 | tf_op jit(solution)/shard_map/ppermute | solution.py:50
  41.5 2.2 %collective-permute-start.14 = (bf16[256,1024]{1,0:T(8,128)(2,1)S(1)}, bf16[256,1024]{1,0:T(8,128)(2,1)S(1)}, u32[]{:S(2)}, u32[]{:S(2)}) collective-permute-start(bf16[256,1024]{1,0:T(8,128)(2,1)S(1)} %pad_maximum_fusion.2), channel_id=1, source_target_pairs={{0,1},{1,0},{2,3},{3,2},{4,5},{5,4},{6,7},{7,6},{8,9},{9,8},{10,11... | collective-permute-start | bytes 1572872 | tf_op jit(solution)/shard_map/ppermute | solution.py:50
  43.7 2.3 %collective-permute-start.13 = (bf16[256,1792]{1,0:T(8,128)(2,1)S(1)}, bf16[256,1792]{1,0:T(8,128)(2,1)S(1)}, u32[]{:S(2)}, u32[]{:S(2)}) collective-permute-start(bf16[256,1792]{1,0:T(8,128)(2,1)S(1)} %bitcast.72), channel_id=1, source_target_pairs={{0,1},{1,0},{2,3},{3,2},{4,5},{5,4},{6,7},{7,6},{8,9},{9,8},{10,11... | collective-permute-start | bytes 2752520 | tf_op jit(solution)/shard_map/ppermute | solution.py:50
  46.7 3.2 %collective-permute-done.11 = f32[16384]{0:T(1024)S(1)} collective-permute-done((f32[16384]{0:T(1024)S(1)}, f32[16384]{0:T(1024)S(1)}, u32[]{:S(2)}, u32[]{:S(2)}) %collective-permute-start.11) | collective-permute-done | bytes 65568 | tf_op jit(solution)/shard_map/ppermute | solution.py:50
  49.9 2.2 %collective-permute-start.12 = (f32[16384]{0:T(1024)S(1)}, f32[16384]{0:T(1024)S(1)}, u32[]{:S(2)}, u32[]{:S(2)}) collective-permute-start(f32[16384]{0:T(1024)S(1)} %add.366), channel_id=1, source_target_pairs={{0,64},{8,72},{16,80},{24,88},{32,96},{40,104},{48,112},{56,120},{... | collective-permute-start | bytes 196616 | tf_op jit(solution)/shard_map/ppermute | solution.py:50
  55.8 2.1 %collective-permute-start.18 = (bf16[128,1792]{1,0:T(8,128)(2,1)S(1)}, bf16[128,1792]{1,0:T(8,128)(2,1)S(1)}, u32[]{:S(2)}, u32[]{:S(2)}) collective-permute-start(bf16[128,1792]{1,0:T(8,128)(2,1)S(1)} %collective-permute-done.6), channel_id=1, source_target_pairs={{0,1},{1,0},{2,3},{3,2},{4,5},{5,4},{6,7},{7,6},{8,9},{9,8},{10,11... | collective-permute-start | bytes 1376264 | tf_op jit(solution)/shard_map/ppermute | solution.py:50
  57.8 5.1 %collective-permute-done.19 = bf16[128,1792]{1,0:T(8,128)(2,1)S(1)} collective-permute-done((bf16[128,1792]{1,0:T(8,128)(2,1)S(1)}, bf16[128,1792]{1,0:T(8,128)(2,1)S(1)}, u32[]{:S(2)}, u32[]{:S(2)}) %collective-permute-start.19) | collective-permute-done | bytes 458784 | tf_op jit(solution)/shard_map/ppermute | solution.py:80
  63.0 2.9 %collective-permute-start.20 = (bf16[128,1792]{1,0:T(8,128)(2,1)S(1)}, bf16[128,1792]{1,0:T(8,128)(2,1)S(1)}, u32[]{:S(2)}, u32[]{:S(2)}) collective-permute-start(bf16[128,1792]{1,0:T(8,128)(2,1)S(1)} %collective-permute-done.19), channel_id=1, source_target_pairs={{0,1},{1,0},{2,3},{3,2},{4,5},{5,4},{6,7},{7,6},{8,9},{9,8},{10,11... | collective-permute-start | bytes 1376264 | tf_op jit(solution)/shard_map/ppermute | solution.py:50
  68.4 4.3 %collective-permute-done.10 = bf16[128,1792]{1,0:T(8,128)(2,1)S(1)} collective-permute-done((bf16[128,1792]{1,0:T(8,128)(2,1)S(1)}, bf16[128,1792]{1,0:T(8,128)(2,1)S(1)}, u32[]{:S(2)}, u32[]{:S(2)}) %collective-permute-start.10) | collective-permute-done | bytes 458784 | tf_op jit(solution)/shard_map/ppermute | solution.py:80
  72.8 1.7 %collective-permute-start.21 = (bf16[128,1792]{1,0:T(8,128)(2,1)S(1)}, bf16[128,1792]{1,0:T(8,128)(2,1)S(1)}, u32[]{:S(2)}, u32[]{:S(2)}) collective-permute-start(bf16[128,1792]{1,0:T(8,128)(2,1)S(1)} %collective-permute-done.10), channel_id=1, source_target_pairs={{0,1},{1,0},{2,3},{3,2},{4,5},{5,4},{6,7},{7,6},{8,9},{9,8},{10,11... | collective-permute-start | bytes 1376264 | tf_op jit(solution)/shard_map/ppermute | solution.py:50
  81.0 5.3 %collective-permute-start.30 = (bf16[16384]{0:T(1024)(128)(2,1)S(1)}, bf16[16384]{0:T(1024)(128)(2,1)S(1)}, u32[]{:S(2)}, u32[]{:S(2)}) collective-permute-start(bf16[16384]{0:T(1024)(128)(2,1)S(1)} %add.367), channel_id=1, source_target_pairs={{0,128},{8,136},{16,144},{24,152},{32,160},{40,168},{48,176},{56,1... | collective-permute-start | bytes 98312 | tf_op jit(solution)/shard_map/ppermute | solution.py:50
  88.4 5.7 %collective-permute-done.23 = bf16[256,896]{1,0:T(8,128)(2,1)S(1)} collective-permute-done((bf16[256,896]{1,0:T(8,128)(2,1)S(1)}, bf16[256,896]{1,0:T(8,128)(2,1)S(1)}, u32[]{:S(2)}, u32[]{:S(2)}) %collective-permute-start.23) | collective-permute-done | bytes 458784 | tf_op jit(solution)/shard_map/ppermute | solution.py:80
  94.7 9.2 %collective-permute-done.26 = bf16[256,896]{1,0:T(8,128)(2,1)S(1)} collective-permute-done((bf16[256,896]{1,0:T(8,128)(2,1)S(1)}, bf16[256,896]{1,0:T(8,128)(2,1)S(1)}, u32[]{:S(2)}, u32[]{:S(2)}) %collective-permute-start.26) | collective-permute-done | bytes 458784 | tf_op jit(solution)/shard_map/ppermute | solution.py:80
  108.4 6.0 %collective-permute-done.25 = bf16[256,896]{1,0:T(8,128)(2,1)S(1)} collective-permute-done((bf16[256,896]{1,0:T(8,128)(2,1)S(1)}, bf16[256,896]{1,0:T(8,128)(2,1)S(1)}, u32[]{:S(2)}, u32[]{:S(2)}) %collective-permute-start.25) | collective-permute-done | bytes 458784 | tf_op jit(solution)/shard_map/ppermute | solution.py:80
  114.9 9.4 %collective-permute-done.28 = bf16[256,896]{1,0:T(8,128)(2,1)S(1)} collective-permute-done((bf16[256,896]{1,0:T(8,128)(2,1)S(1)}, bf16[256,896]{1,0:T(8,128)(2,1)S(1)}, u32[]{:S(2)}, u32[]{:S(2)}) %collective-permute-start.28) | collective-permute-done | bytes 458784 | tf_op jit(solution)/shard_map/ppermute | solution.py:80
  124.7 1.9 %collective-permute-done.31 = bf16[16384]{0:T(1024)(128)(2,1)S(1)} collective-permute-done((bf16[16384]{0:T(1024)(128)(2,1)S(1)}, bf16[16384]{0:T(1024)(128)(2,1)S(1)}, u32[]{:S(2)}, u32[]{:S(2)}) %collective-permute-start.31) | collective-permute-done | bytes 32800 | tf_op jit(solution)/shard_map/ppermute | solution.py:50
  128.5 19.6 %collective-permute-done.32 = bf16[32768]{0:T(1024)(128)(2,1)S(1)} collective-permute-done((bf16[32768]{0:T(1024)(128)(2,1)S(1)}, bf16[32768]{0:T(1024)(128)(2,1)S(1)}, u32[]{:S(2)}, u32[]{:S(2)}) %collective-permute-start.32) | collective-permute-done | bytes 65568 | tf_op jit(solution)/shard_map/ppermute | solution.py:50
  152.2 3.1 %fusion.2 = (bf16[1,256,1792]{2,1,0:T(8,128)(2,1)}, f32[1,256,1792]{2,1,0:T(8,128)}, f32[1,256,1792]{2,1,0:T(8,128)}) fusion(bf16[1,256,1792]{2,1,0:T(8,128)(2,1)S(1)} %copy-done, f32[1,256,896]{2,1,0:T(8,128)S(1)} %fusion.17, f32[1,256,896]{2,1,0:T(8,128)S(1)} %fusion.19, f32[1,256,1792]{2,1,0:T(8,128)S(1)} %copy-done.6, f32[1,256,1792]{2,1,0:T(8,128)S(1)} %copy-done.7), kind=kLoop, calls=%fused_computation.6 | loop fusion | flops 8257536 | bytes 11010048 | tf_op jit(solution)/shard_map/convert_element_type | solution.py:36
  (178 shorter events, 39.5 us)
Async XLA Ops:
  5.4 14.1 %collective-permute-start.2 = (bf16[128,1792]{1,0:T(8,128)(2,1)S(1)}, bf16[128,1792]{1,0:T(8,128)(2,1)}, u32[]{:S(2)}, u32[]{:S(2)}) collective-permute-start(bf16[128,1792]{1,0:T(8,128)(2,1)S(1)} %get-tuple-element.98), channel_id=1, source_target_pairs={{0,2},{1,3},{2,4},{3,5},{4,6},{5,7},{6,0},{7,1},{8,10},{9,11},{10,... | collective-permute-start | bytes 1376264 | tf_op jit(solution)/shard_map/ppermute | solution.py:80
  6.4 22.8 %collective-permute-start.1 = (bf16[128,1792]{1,0:T(8,128)(2,1)S(1)}, bf16[128,1792]{1,0:T(8,128)(2,1)S(1)}, u32[]{:S(2)}, u32[]{:S(2)}) collective-permute-start(bf16[128,1792]{1,0:T(8,128)(2,1)S(1)} %get-tuple-element.44), channel_id=1, source_target_pairs={{0,2},{1,3},{2,4},{3,5},{4,6},{5,7},{6,0},{7,1},{8,10},{9,11},{10,... | collective-permute-start | bytes 1376264 | tf_op jit(solution)/shard_map/ppermute | solution.py:80
  7.3 23.9 %collective-permute-start.3 = (bf16[16384]{0:T(1024)(128)(2,1)S(1)}, bf16[16384]{0:T(1024)(128)(2,1)S(1)}, u32[]{:S(2)}, u32[]{:S(2)}) collective-permute-start(bf16[16384]{0:T(1024)(128)(2,1)S(1)} %get-tuple-element.102), channel_id=1, source_target_pairs={{0,2},{1,3},{2,0},{3,1},{4,6},{5,7},{6,4},{7,5},{8,10},{9,11},{10,... | collective-permute-start | bytes 98312 | tf_op jit(solution)/shard_map/ppermute | solution.py:50
  9.0 22.2 %collective-permute-start.4 = (bf16[16384]{0:T(1024)(128)(2,1)S(1)}, bf16[16384]{0:T(1024)(128)(2,1)S(1)}, u32[]{:S(2)}, u32[]{:S(2)}) collective-permute-start(bf16[16384]{0:T(1024)(128)(2,1)S(1)} %get-tuple-element.101), channel_id=1, source_target_pairs={{0,4},{1,5},{2,6},{3,7},{4,0},{5,1},{6,2},{7,3},{8,12},{9,13},{10,... | collective-permute-start | bytes 98312 | tf_op jit(solution)/shard_map/ppermute | solution.py:50
  10.1 21.1 %collective-permute-start.5 = (bf16[16384]{0:T(1024)(128)(2,1)S(1)}, bf16[16384]{0:T(1024)(128)(2,1)S(1)}, u32[]{:S(2)}, u32[]{:S(2)}) collective-permute-start(bf16[16384]{0:T(1024)(128)(2,1)S(1)} %get-tuple-element.100), channel_id=1, source_target_pairs={{0,6},{1,7},{2,4},{3,5},{4,2},{5,3},{6,0},{7,1},{8,14},{9,15},{10,... | collective-permute-start | bytes 98312 | tf_op jit(solution)/shard_map/ppermute | solution.py:50
  20.6 25.5 %collective-permute-start.15 = (bf16[128,1792]{1,0:T(8,128)(2,1)}, bf16[128,1792]{1,0:T(8,128)(2,1)S(1)}, u32[]{:S(2)}, u32[]{:S(2)}) collective-permute-start(bf16[128,1792]{1,0:T(8,128)(2,1)} %collective-permute-done.2), channel_id=1, source_target_pairs={{0,1},{1,0},{2,3},{3,2},{4,5},{5,4},{6,7},{7,6},{8,9},{9,8},{10,11... | collective-permute-start | bytes 1376264 | tf_op jit(solution)/shard_map/ppermute | solution.py:50
  29.2 14.5 %collective-permute-start.7 = (bf16[128,1792]{1,0:T(8,128)(2,1)}, bf16[128,1792]{1,0:T(8,128)(2,1)S(1)}, u32[]{:S(2)}, u32[]{:S(2)}) collective-permute-start(bf16[128,1792]{1,0:T(8,128)(2,1)} %collective-permute-done.2), channel_id=1, source_target_pairs={{0,2},{1,3},{2,4},{3,5},{4,6},{5,7},{6,0},{7,1},{8,10},{9,11},{10,... | collective-permute-start | bytes 1376264 | tf_op jit(solution)/shard_map/ppermute | solution.py:80
  31.2 18.7 %collective-permute-start.16 = (bf16[128,1792]{1,0:T(8,128)(2,1)S(1)}, bf16[128,1792]{1,0:T(8,128)(2,1)S(1)}, u32[]{:S(2)}, u32[]{:S(2)}) collective-permute-start(bf16[128,1792]{1,0:T(8,128)(2,1)S(1)} %collective-permute-done.1), channel_id=1, source_target_pairs={{0,1},{1,0},{2,3},{3,2},{4,5},{5,4},{6,7},{7,6},{8,9},{9,8},{10,11... | collective-permute-start | bytes 1376264 | tf_op jit(solution)/shard_map/ppermute | solution.py:50
  32.3 21.1 %collective-permute-start.6 = (bf16[128,1792]{1,0:T(8,128)(2,1)S(1)}, bf16[128,1792]{1,0:T(8,128)(2,1)S(1)}, u32[]{:S(2)}, u32[]{:S(2)}) collective-permute-start(bf16[128,1792]{1,0:T(8,128)(2,1)S(1)} %collective-permute-done.1), channel_id=1, source_target_pairs={{0,2},{1,3},{2,4},{3,5},{4,6},{5,7},{6,0},{7,1},{8,10},{9,11},{10,... | collective-permute-start | bytes 1376264 | tf_op jit(solution)/shard_map/ppermute | solution.py:80
  41.5 14.2 %collective-permute-start.14 = (bf16[256,1024]{1,0:T(8,128)(2,1)S(1)}, bf16[256,1024]{1,0:T(8,128)(2,1)S(1)}, u32[]{:S(2)}, u32[]{:S(2)}) collective-permute-start(bf16[256,1024]{1,0:T(8,128)(2,1)S(1)} %pad_maximum_fusion.2), channel_id=1, source_target_pairs={{0,1},{1,0},{2,3},{3,2},{4,5},{5,4},{6,7},{7,6},{8,9},{9,8},{10,11... | collective-permute-start | bytes 1572872 | tf_op jit(solution)/shard_map/ppermute | solution.py:50
  43.7 11.1 %collective-permute-start.13 = (bf16[256,1792]{1,0:T(8,128)(2,1)S(1)}, bf16[256,1792]{1,0:T(8,128)(2,1)S(1)}, u32[]{:S(2)}, u32[]{:S(2)}) collective-permute-start(bf16[256,1792]{1,0:T(8,128)(2,1)S(1)} %bitcast.72), channel_id=1, source_target_pairs={{0,1},{1,0},{2,3},{3,2},{4,5},{5,4},{6,7},{7,6},{8,9},{9,8},{10,11... | collective-permute-start | bytes 2752520 | tf_op jit(solution)/shard_map/ppermute | solution.py:50
  49.9 13.1 %collective-permute-start.19 = (bf16[128,1792]{1,0:T(8,128)(2,1)S(1)}, bf16[128,1792]{1,0:T(8,128)(2,1)S(1)}, u32[]{:S(2)}, u32[]{:S(2)}) collective-permute-start(bf16[128,1792]{1,0:T(8,128)(2,1)S(1)} %collective-permute-done.7), channel_id=1, source_target_pairs={{0,2},{1,3},{2,4},{3,5},{4,6},{5,7},{6,0},{7,1},{8,10},{9,11},{10,... | collective-permute-start | bytes 1376264 | tf_op jit(solution)/shard_map/ppermute | solution.py:80
  53.4 12.6 %collective-permute-start.17 = (bf16[128,1792]{1,0:T(8,128)(2,1)S(1)}, bf16[128,1792]{1,0:T(8,128)(2,1)S(1)}, u32[]{:S(2)}, u32[]{:S(2)}) collective-permute-start(bf16[128,1792]{1,0:T(8,128)(2,1)S(1)} %collective-permute-done.7), channel_id=1, source_target_pairs={{0,1},{1,0},{2,3},{3,2},{4,5},{5,4},{6,7},{7,6},{8,9},{9,8},{10,11... | collective-permute-start | bytes 1376264 | tf_op jit(solution)/shard_map/ppermute | solution.py:50
  54.6 18.2 %collective-permute-start.10 = (bf16[128,1792]{1,0:T(8,128)(2,1)S(1)}, bf16[128,1792]{1,0:T(8,128)(2,1)S(1)}, u32[]{:S(2)}, u32[]{:S(2)}) collective-permute-start(bf16[128,1792]{1,0:T(8,128)(2,1)S(1)} %collective-permute-done.6), channel_id=1, source_target_pairs={{0,2},{1,3},{2,4},{3,5},{4,6},{5,7},{6,0},{7,1},{8,10},{9,11},{10,... | collective-permute-start | bytes 1376264 | tf_op jit(solution)/shard_map/ppermute | solution.py:80
  55.8 10.6 %collective-permute-start.18 = (bf16[128,1792]{1,0:T(8,128)(2,1)S(1)}, bf16[128,1792]{1,0:T(8,128)(2,1)S(1)}, u32[]{:S(2)}, u32[]{:S(2)}) collective-permute-start(bf16[128,1792]{1,0:T(8,128)(2,1)S(1)} %collective-permute-done.6), channel_id=1, source_target_pairs={{0,1},{1,0},{2,3},{3,2},{4,5},{5,4},{6,7},{7,6},{8,9},{9,8},{10,11... | collective-permute-start | bytes 1376264 | tf_op jit(solution)/shard_map/ppermute | solution.py:50
  79.7 14.3 %collective-permute-start.23 = (bf16[256,896]{1,0:T(8,128)(2,1)S(1)}, bf16[256,896]{1,0:T(8,128)(2,1)S(1)}, u32[]{:S(2)}, u32[]{:S(2)}) collective-permute-start(bf16[256,896]{1,0:T(8,128)(2,1)S(1)} %fusion.24), channel_id=1, source_target_pairs={{0,2},{1,3},{2,4},{3,5},{4,6},{5,7},{6,0},{7,1},{8,10},{9,11},{10,... | collective-permute-start | bytes 1376264 | tf_op jit(solution)/shard_map/ppermute | solution.py:80
  80.9 23.0 %collective-permute-start.26 = (bf16[256,896]{1,0:T(8,128)(2,1)S(1)}, bf16[256,896]{1,0:T(8,128)(2,1)S(1)}, u32[]{:S(2)}, u32[]{:S(2)}) collective-permute-start(bf16[256,896]{1,0:T(8,128)(2,1)S(1)} %fusion.25), channel_id=1, source_target_pairs={{0,2},{1,3},{2,4},{3,5},{4,6},{5,7},{6,0},{7,1},{8,10},{9,11},{10,... | collective-permute-start | bytes 1376264 | tf_op jit(solution)/shard_map/ppermute | solution.py:80
  81.0 25.6 %collective-permute-start.30 = (bf16[16384]{0:T(1024)(128)(2,1)S(1)}, bf16[16384]{0:T(1024)(128)(2,1)S(1)}, u32[]{:S(2)}, u32[]{:S(2)}) collective-permute-start(bf16[16384]{0:T(1024)(128)(2,1)S(1)} %add.367), channel_id=1, source_target_pairs={{0,128},{8,136},{16,144},{24,152},{32,160},{40,168},{48,176},{56,1... | collective-permute-start | bytes 98312 | tf_op jit(solution)/shard_map/ppermute | solution.py:50
  94.4 20.0 %collective-permute-start.25 = (bf16[256,896]{1,0:T(8,128)(2,1)S(1)}, bf16[256,896]{1,0:T(8,128)(2,1)S(1)}, u32[]{:S(2)}, u32[]{:S(2)}) collective-permute-start(bf16[256,896]{1,0:T(8,128)(2,1)S(1)} %fusion.26), channel_id=1, source_target_pairs={{0,2},{1,3},{2,4},{3,5},{4,6},{5,7},{6,0},{7,1},{8,10},{9,11},{10,... | collective-permute-start | bytes 1376264 | tf_op jit(solution)/shard_map/ppermute | solution.py:80
  104.2 20.0 %collective-permute-start.28 = (bf16[256,896]{1,0:T(8,128)(2,1)S(1)}, bf16[256,896]{1,0:T(8,128)(2,1)S(1)}, u32[]{:S(2)}, u32[]{:S(2)}) collective-permute-start(bf16[256,896]{1,0:T(8,128)(2,1)S(1)} %fusion.27), channel_id=1, source_target_pairs={{0,2},{1,3},{2,4},{3,5},{4,6},{5,7},{6,0},{7,1},{8,10},{9,11},{10,... | collective-permute-start | bytes 1376264 | tf_op jit(solution)/shard_map/ppermute | solution.py:80
  106.6 20.0 %collective-permute-start.31 = (bf16[16384]{0:T(1024)(128)(2,1)S(1)}, bf16[16384]{0:T(1024)(128)(2,1)S(1)}, u32[]{:S(2)}, u32[]{:S(2)}) collective-permute-start(bf16[16384]{0:T(1024)(128)(2,1)S(1)} %get-tuple-element.82), channel_id=1, source_target_pairs={{0,2},{1,3},{2,0},{3,1},{4,6},{5,7},{6,4},{7,5},{8,10},{9,11},{10,... | collective-permute-start | bytes 98312 | tf_op jit(solution)/shard_map/ppermute | solution.py:50
  114.8 35.1 %collective-permute-start.27 = (bf16[256,896]{1,0:T(8,128)(2,1)S(1)}, bf16[256,896]{1,0:T(8,128)(2,1)S(1)}, u32[]{:S(2)}, u32[]{:S(2)}) collective-permute-start(bf16[256,896]{1,0:T(8,128)(2,1)S(1)} %fusion.28), channel_id=1, source_target_pairs={{0,2},{1,3},{2,4},{3,5},{4,6},{5,7},{6,0},{7,1},{8,10},{9,11},{10,... | collective-permute-start | bytes 1376264 | tf_op jit(solution)/shard_map/ppermute | solution.py:80
  124.6 25.3 %collective-permute-start.29 = (bf16[256,896]{1,0:T(8,128)(2,1)S(1)}, bf16[256,896]{1,0:T(8,128)(2,1)S(1)}, u32[]{:S(2)}, u32[]{:S(2)}) collective-permute-start(bf16[256,896]{1,0:T(8,128)(2,1)S(1)} %fusion.29), channel_id=1, source_target_pairs={{0,2},{1,3},{2,4},{3,5},{4,6},{5,7},{6,0},{7,1},{8,10},{9,11},{10,... | collective-permute-start | bytes 1376264 | tf_op jit(solution)/shard_map/ppermute | solution.py:80
  126.6 21.6 %collective-permute-start.32 = (bf16[32768]{0:T(1024)(128)(2,1)S(1)}, bf16[32768]{0:T(1024)(128)(2,1)S(1)}, u32[]{:S(2)}, u32[]{:S(2)}) collective-permute-start(bf16[32768]{0:T(1024)(128)(2,1)S(1)} %pad_maximum_fusion.5), channel_id=1, source_target_pairs={{0,4},{1,5},{2,6},{3,7},{4,0},{5,1},{6,2},{7,3},{8,12},{9,13},{10,... | collective-permute-start | bytes 196616 | tf_op jit(solution)/shard_map/ppermute | solution.py:50
  (37 other events, 203.1 us)

commit v4 on v3

--- a/solution.py
+++ b/solution.py
@@ -27,12 +27,11 @@
 def adamw(weight, moment, second, gradient):
     moment_new = beta_one * moment + (1.0 - beta_one) * gradient
     second_new = beta_two * second + (1.0 - beta_two) * gradient * gradient
-    moment_hat = moment_new / (1.0 - beta_one**inner_step)
-    second_hat = second_new / (1.0 - beta_two**inner_step)
+    moment_hat = moment_new * (inner_rate / (1.0 - beta_one**inner_step))
+    second_hat = second_new * (1.0 / (1.0 - beta_two**inner_step))
     master = weight.astype(jnp.float32)
-    updated = master - inner_rate * (
-        moment_hat / (jnp.sqrt(second_hat) + adam_eps) + decay_rate * master
-    )
+    step = moment_hat / (jnp.sqrt(second_hat) + adam_eps)
+    updated = master * (1.0 - inner_rate * decay_rate) - step
     return (updated.astype(jnp.bfloat16), moment_new, second_new)
 
 

time: 156 us -> 156 us (level)
  no operation moved by 1% of the time
where the time goes in v4:
time: 156 us; the launch traced here: 155 us
  waiting for transfers between devices  89.8 us (58%)
  starting transfers between devices  36.9 us (24%)
  matrix products  13.1 us (8%)
  local copies, waits for them, and re-layouts  8.08 us (5%)
  other arithmetic  5 us (3%)
  between operations  2.35 us (2%)
    ppermute x12, waiting for transfers between devices, send(): return lax.ppermute(value, 'node', pairs)  55.2 us
    ppermute x22, waiting for transfers between devices, swapped(): return lax.ppermute(value, axis, [(a, a ^ mask) for a in range(size)])  34.6 us
    ppermute x22, starting transfers between devices, swapped(): return lax.ppermute(value, axis, [(a, a ^ mask) for a in range(size)])  34.3 us
    unnamed x60, local copies, waits for them, and re-layouts  5.86 us
    dot_general x8, matrix products, product(): return total + jnp.dot(left, right, preferred_element_type=f32)  5.18 us
  transfers between devices with their start and end apart: 34, of which 21 were waited for; matrix products, arithmetic and copies ran while one was open for 10% of the time, Pallas kernels for 0%

profile of v4, /device:TPU:1, one launch (start us, length us, event | category | flops | bytes accessed | tf_op | source)
XLA Modules:
  0.0 155.3 jit_solution(15692224176290755994)
XLA Ops:
  2.1 3.3 %collective-permute-start = (bf16[65536]{0:T(1024)(128)(2,1)S(1)}, bf16[65536]{0:T(1024)(128)(2,1)S(1)}, u32[]{:S(2)}, u32[]{:S(2)}) collective-permute-start(bf16[65536]{0:T(1024)(128)(2,1)S(1)} %pad_maximum_fusion.3), channel_id=1, source_target_pairs={{0,1},{1,0},{2,3},{3,2},{4,5},{5,4},{6,7},{7,6},{8,9},{9,8},{10,11... | collective-permute-start | bytes 393224 | tf_op jit(solution)/shard_map/ppermute | solution.py:49
  7.3 1.7 %collective-permute-start.3 = (bf16[16384]{0:T(1024)(128)(2,1)S(1)}, bf16[16384]{0:T(1024)(128)(2,1)S(1)}, u32[]{:S(2)}, u32[]{:S(2)}) collective-permute-start(bf16[16384]{0:T(1024)(128)(2,1)S(1)} %get-tuple-element.102), channel_id=1, source_target_pairs={{0,2},{1,3},{2,0},{3,1},{4,6},{5,7},{6,4},{7,5},{8,10},{9,11},{10,... | collective-permute-start | bytes 98312 | tf_op jit(solution)/shard_map/ppermute | solution.py:49
  11.2 8.3 %collective-permute-done.2 = bf16[128,1792]{1,0:T(8,128)(2,1)} collective-permute-done((bf16[128,1792]{1,0:T(8,128)(2,1)S(1)}, bf16[128,1792]{1,0:T(8,128)(2,1)}, u32[]{:S(2)}, u32[]{:S(2)}) %collective-permute-start.2) | collective-permute-done | bytes 458784 | tf_op jit(solution)/shard_map/ppermute | solution.py:79
  22.1 7.1 %collective-permute-done.1 = bf16[128,1792]{1,0:T(8,128)(2,1)S(1)} collective-permute-done((bf16[128,1792]{1,0:T(8,128)(2,1)S(1)}, bf16[128,1792]{1,0:T(8,128)(2,1)S(1)}, u32[]{:S(2)}, u32[]{:S(2)}) %collective-permute-start.1) | collective-permute-done | bytes 458784 | tf_op jit(solution)/shard_map/ppermute | solution.py:79
  29.2 1.9 %collective-permute-done.3 = bf16[16384]{0:T(1024)(128)(2,1)S(1)} collective-permute-done((bf16[16384]{0:T(1024)(128)(2,1)S(1)}, bf16[16384]{0:T(1024)(128)(2,1)S(1)}, u32[]{:S(2)}, u32[]{:S(2)}) %collective-permute-start.3) | collective-permute-done | bytes 32800 | tf_op jit(solution)/shard_map/ppermute | solution.py:49
  36.7 2.2 %collective-permute-start.9 = (f32[16384]{0:T(1024)S(1)}, f32[16384]{0:T(1024)S(1)}, u32[]{:S(2)}, u32[]{:S(2)}) collective-permute-start(f32[16384]{0:T(1024)S(1)} %add.360), channel_id=1, source_target_pairs={{0,16},{8,24},{16,0},{24,8},{32,48},{40,56},{48,32},{56,40},{64,80... | collective-permute-start | bytes 196616 | tf_op jit(solution)/shard_map/ppermute | solution.py:49
  38.9 2.6 %collective-permute-done.9 = f32[16384]{0:T(1024)S(1)} collective-permute-done((f32[16384]{0:T(1024)S(1)}, f32[16384]{0:T(1024)S(1)}, u32[]{:S(2)}, u32[]{:S(2)}) %collective-permute-start.9) | collective-permute-done | bytes 65568 | tf_op jit(solution)/shard_map/ppermute | solution.py:49
  41.5 2.2 %collective-permute-start.14 = (bf16[256,1024]{1,0:T(8,128)(2,1)S(1)}, bf16[256,1024]{1,0:T(8,128)(2,1)S(1)}, u32[]{:S(2)}, u32[]{:S(2)}) collective-permute-start(bf16[256,1024]{1,0:T(8,128)(2,1)S(1)} %pad_maximum_fusion.2), channel_id=1, source_target_pairs={{0,1},{1,0},{2,3},{3,2},{4,5},{5,4},{6,7},{7,6},{8,9},{9,8},{10,11... | collective-permute-start | bytes 1572872 | tf_op jit(solution)/shard_map/ppermute | solution.py:49
  43.7 2.3 %collective-permute-start.13 = (bf16[256,1792]{1,0:T(8,128)(2,1)S(1)}, bf16[256,1792]{1,0:T(8,128)(2,1)S(1)}, u32[]{:S(2)}, u32[]{:S(2)}) collective-permute-start(bf16[256,1792]{1,0:T(8,128)(2,1)S(1)} %bitcast.72), channel_id=1, source_target_pairs={{0,1},{1,0},{2,3},{3,2},{4,5},{5,4},{6,7},{7,6},{8,9},{9,8},{10,11... | collective-permute-start | bytes 2752520 | tf_op jit(solution)/shard_map/ppermute | solution.py:49
  46.7 3.2 %collective-permute-done.11 = f32[16384]{0:T(1024)S(1)} collective-permute-done((f32[16384]{0:T(1024)S(1)}, f32[16384]{0:T(1024)S(1)}, u32[]{:S(2)}, u32[]{:S(2)}) %collective-permute-start.11) | collective-permute-done | bytes 65568 | tf_op jit(solution)/shard_map/ppermute | solution.py:49
  49.9 2.2 %collective-permute-start.12 = (f32[16384]{0:T(1024)S(1)}, f32[16384]{0:T(1024)S(1)}, u32[]{:S(2)}, u32[]{:S(2)}) collective-permute-start(f32[16384]{0:T(1024)S(1)} %add.362), channel_id=1, source_target_pairs={{0,64},{8,72},{16,80},{24,88},{32,96},{40,104},{48,112},{56,120},{... | collective-permute-start | bytes 196616 | tf_op jit(solution)/shard_map/ppermute | solution.py:49
  55.8 2.1 %collective-permute-start.18 = (bf16[128,1792]{1,0:T(8,128)(2,1)S(1)}, bf16[128,1792]{1,0:T(8,128)(2,1)S(1)}, u32[]{:S(2)}, u32[]{:S(2)}) collective-permute-start(bf16[128,1792]{1,0:T(8,128)(2,1)S(1)} %collective-permute-done.6), channel_id=1, source_target_pairs={{0,1},{1,0},{2,3},{3,2},{4,5},{5,4},{6,7},{7,6},{8,9},{9,8},{10,11... | collective-permute-start | bytes 1376264 | tf_op jit(solution)/shard_map/ppermute | solution.py:49
  57.8 5.1 %collective-permute-done.19 = bf16[128,1792]{1,0:T(8,128)(2,1)S(1)} collective-permute-done((bf16[128,1792]{1,0:T(8,128)(2,1)S(1)}, bf16[128,1792]{1,0:T(8,128)(2,1)S(1)}, u32[]{:S(2)}, u32[]{:S(2)}) %collective-permute-start.19) | collective-permute-done | bytes 458784 | tf_op jit(solution)/shard_map/ppermute | solution.py:79
  63.0 2.9 %collective-permute-start.20 = (bf16[128,1792]{1,0:T(8,128)(2,1)S(1)}, bf16[128,1792]{1,0:T(8,128)(2,1)S(1)}, u32[]{:S(2)}, u32[]{:S(2)}) collective-permute-start(bf16[128,1792]{1,0:T(8,128)(2,1)S(1)} %collective-permute-done.19), channel_id=1, source_target_pairs={{0,1},{1,0},{2,3},{3,2},{4,5},{5,4},{6,7},{7,6},{8,9},{9,8},{10,11... | collective-permute-start | bytes 1376264 | tf_op jit(solution)/shard_map/ppermute | solution.py:49
  68.4 4.3 %collective-permute-done.10 = bf16[128,1792]{1,0:T(8,128)(2,1)S(1)} collective-permute-done((bf16[128,1792]{1,0:T(8,128)(2,1)S(1)}, bf16[128,1792]{1,0:T(8,128)(2,1)S(1)}, u32[]{:S(2)}, u32[]{:S(2)}) %collective-permute-start.10) | collective-permute-done | bytes 458784 | tf_op jit(solution)/shard_map/ppermute | solution.py:79
  72.8 1.7 %collective-permute-start.21 = (bf16[128,1792]{1,0:T(8,128)(2,1)S(1)}, bf16[128,1792]{1,0:T(8,128)(2,1)S(1)}, u32[]{:S(2)}, u32[]{:S(2)}) collective-permute-start(bf16[128,1792]{1,0:T(8,128)(2,1)S(1)} %collective-permute-done.10), channel_id=1, source_target_pairs={{0,1},{1,0},{2,3},{3,2},{4,5},{5,4},{6,7},{7,6},{8,9},{9,8},{10,11... | collective-permute-start | bytes 1376264 | tf_op jit(solution)/shard_map/ppermute | solution.py:49
  81.0 5.3 %collective-permute-start.30 = (bf16[16384]{0:T(1024)(128)(2,1)S(1)}, bf16[16384]{0:T(1024)(128)(2,1)S(1)}, u32[]{:S(2)}, u32[]{:S(2)}) collective-permute-start(bf16[16384]{0:T(1024)(128)(2,1)S(1)} %add.363), channel_id=1, source_target_pairs={{0,128},{8,136},{16,144},{24,152},{32,160},{40,168},{48,176},{56,1... | collective-permute-start | bytes 98312 | tf_op jit(solution)/shard_map/ppermute | solution.py:49
  88.4 5.7 %collective-permute-done.23 = bf16[256,896]{1,0:T(8,128)(2,1)S(1)} collective-permute-done((bf16[256,896]{1,0:T(8,128)(2,1)S(1)}, bf16[256,896]{1,0:T(8,128)(2,1)S(1)}, u32[]{:S(2)}, u32[]{:S(2)}) %collective-permute-start.23) | collective-permute-done | bytes 458784 | tf_op jit(solution)/shard_map/ppermute | solution.py:79
  94.7 9.2 %collective-permute-done.26 = bf16[256,896]{1,0:T(8,128)(2,1)S(1)} collective-permute-done((bf16[256,896]{1,0:T(8,128)(2,1)S(1)}, bf16[256,896]{1,0:T(8,128)(2,1)S(1)}, u32[]{:S(2)}, u32[]{:S(2)}) %collective-permute-start.26) | collective-permute-done | bytes 458784 | tf_op jit(solution)/shard_map/ppermute | solution.py:79
  108.4 6.0 %collective-permute-done.25 = bf16[256,896]{1,0:T(8,128)(2,1)S(1)} collective-permute-done((bf16[256,896]{1,0:T(8,128)(2,1)S(1)}, bf16[256,896]{1,0:T(8,128)(2,1)S(1)}, u32[]{:S(2)}, u32[]{:S(2)}) %collective-permute-start.25) | collective-permute-done | bytes 458784 | tf_op jit(solution)/shard_map/ppermute | solution.py:79
  114.9 9.4 %collective-permute-done.28 = bf16[256,896]{1,0:T(8,128)(2,1)S(1)} collective-permute-done((bf16[256,896]{1,0:T(8,128)(2,1)S(1)}, bf16[256,896]{1,0:T(8,128)(2,1)S(1)}, u32[]{:S(2)}, u32[]{:S(2)}) %collective-permute-start.28) | collective-permute-done | bytes 458784 | tf_op jit(solution)/shard_map/ppermute | solution.py:79
  124.7 1.9 %collective-permute-done.31 = bf16[16384]{0:T(1024)(128)(2,1)S(1)} collective-permute-done((bf16[16384]{0:T(1024)(128)(2,1)S(1)}, bf16[16384]{0:T(1024)(128)(2,1)S(1)}, u32[]{:S(2)}, u32[]{:S(2)}) %collective-permute-start.31) | collective-permute-done | bytes 32800 | tf_op jit(solution)/shard_map/ppermute | solution.py:49
  128.5 19.6 %collective-permute-done.32 = bf16[32768]{0:T(1024)(128)(2,1)S(1)} collective-permute-done((bf16[32768]{0:T(1024)(128)(2,1)S(1)}, bf16[32768]{0:T(1024)(128)(2,1)S(1)}, u32[]{:S(2)}, u32[]{:S(2)}) %collective-permute-start.32) | collective-permute-done | bytes 65568 | tf_op jit(solution)/shard_map/ppermute | solution.py:49
  152.2 3.1 %subtract_convert_fusion = (bf16[1,256,1792]{2,1,0:T(8,128)(2,1)}, f32[1,256,1792]{2,1,0:T(8,128)}, f32[1,256,1792]{2,1,0:T(8,128)}) fusion(bf16[1,256,1792]{2,1,0:T(8,128)(2,1)S(1)} %copy-done, f32[1,256,896]{2,1,0:T(8,128)S(1)} %fusion.14, f32[1,256,896]{2,1,0:T(8,128)S(1)} %fusion.16, f32[1,256,1792]{2,1,0:T(8,128)S(1)} %copy-done.6, ...), kind=kLoop, calls=%fused_computation.16 | loop fusion | flops 7340032 | bytes 11010048 | tf_op jit(solution)/shard_map/convert_element_type | solution.py:35
  (178 shorter events, 39.5 us)
Async XLA Ops:
  5.4 14.1 %collective-permute-start.2 = (bf16[128,1792]{1,0:T(8,128)(2,1)S(1)}, bf16[128,1792]{1,0:T(8,128)(2,1)}, u32[]{:S(2)}, u32[]{:S(2)}) collective-permute-start(bf16[128,1792]{1,0:T(8,128)(2,1)S(1)} %get-tuple-element.98), channel_id=1, source_target_pairs={{0,2},{1,3},{2,4},{3,5},{4,6},{5,7},{6,0},{7,1},{8,10},{9,11},{10,... | collective-permute-start | bytes 1376264 | tf_op jit(solution)/shard_map/ppermute | solution.py:79
  6.4 22.8 %collective-permute-start.1 = (bf16[128,1792]{1,0:T(8,128)(2,1)S(1)}, bf16[128,1792]{1,0:T(8,128)(2,1)S(1)}, u32[]{:S(2)}, u32[]{:S(2)}) collective-permute-start(bf16[128,1792]{1,0:T(8,128)(2,1)S(1)} %get-tuple-element.44), channel_id=1, source_target_pairs={{0,2},{1,3},{2,4},{3,5},{4,6},{5,7},{6,0},{7,1},{8,10},{9,11},{10,... | collective-permute-start | bytes 1376264 | tf_op jit(solution)/shard_map/ppermute | solution.py:79
  7.3 23.9 %collective-permute-start.3 = (bf16[16384]{0:T(1024)(128)(2,1)S(1)}, bf16[16384]{0:T(1024)(128)(2,1)S(1)}, u32[]{:S(2)}, u32[]{:S(2)}) collective-permute-start(bf16[16384]{0:T(1024)(128)(2,1)S(1)} %get-tuple-element.102), channel_id=1, source_target_pairs={{0,2},{1,3},{2,0},{3,1},{4,6},{5,7},{6,4},{7,5},{8,10},{9,11},{10,... | collective-permute-start | bytes 98312 | tf_op jit(solution)/shard_map/ppermute | solution.py:49
  9.0 22.2 %collective-permute-start.4 = (bf16[16384]{0:T(1024)(128)(2,1)S(1)}, bf16[16384]{0:T(1024)(128)(2,1)S(1)}, u32[]{:S(2)}, u32[]{:S(2)}) collective-permute-start(bf16[16384]{0:T(1024)(128)(2,1)S(1)} %get-tuple-element.101), channel_id=1, source_target_pairs={{0,4},{1,5},{2,6},{3,7},{4,0},{5,1},{6,2},{7,3},{8,12},{9,13},{10,... | collective-permute-start | bytes 98312 | tf_op jit(solution)/shard_map/ppermute | solution.py:49
  10.1 21.1 %collective-permute-start.5 = (bf16[16384]{0:T(1024)(128)(2,1)S(1)}, bf16[16384]{0:T(1024)(128)(2,1)S(1)}, u32[]{:S(2)}, u32[]{:S(2)}) collective-permute-start(bf16[16384]{0:T(1024)(128)(2,1)S(1)} %get-tuple-element.100), channel_id=1, source_target_pairs={{0,6},{1,7},{2,4},{3,5},{4,2},{5,3},{6,0},{7,1},{8,14},{9,15},{10,... | collective-permute-start | bytes 98312 | tf_op jit(solution)/shard_map/ppermute | solution.py:49
  20.6 25.5 %collective-permute-start.15 = (bf16[128,1792]{1,0:T(8,128)(2,1)}, bf16[128,1792]{1,0:T(8,128)(2,1)S(1)}, u32[]{:S(2)}, u32[]{:S(2)}) collective-permute-start(bf16[128,1792]{1,0:T(8,128)(2,1)} %collective-permute-done.2), channel_id=1, source_target_pairs={{0,1},{1,0},{2,3},{3,2},{4,5},{5,4},{6,7},{7,6},{8,9},{9,8},{10,11... | collective-permute-start | bytes 1376264 | tf_op jit(solution)/shard_map/ppermute | solution.py:49
  29.2 14.5 %collective-permute-start.7 = (bf16[128,1792]{1,0:T(8,128)(2,1)}, bf16[128,1792]{1,0:T(8,128)(2,1)S(1)}, u32[]{:S(2)}, u32[]{:S(2)}) collective-permute-start(bf16[128,1792]{1,0:T(8,128)(2,1)} %collective-permute-done.2), channel_id=1, source_target_pairs={{0,2},{1,3},{2,4},{3,5},{4,6},{5,7},{6,0},{7,1},{8,10},{9,11},{10,... | collective-permute-start | bytes 1376264 | tf_op jit(solution)/shard_map/ppermute | solution.py:79
  31.2 18.7 %collective-permute-start.16 = (bf16[128,1792]{1,0:T(8,128)(2,1)S(1)}, bf16[128,1792]{1,0:T(8,128)(2,1)S(1)}, u32[]{:S(2)}, u32[]{:S(2)}) collective-permute-start(bf16[128,1792]{1,0:T(8,128)(2,1)S(1)} %collective-permute-done.1), channel_id=1, source_target_pairs={{0,1},{1,0},{2,3},{3,2},{4,5},{5,4},{6,7},{7,6},{8,9},{9,8},{10,11... | collective-permute-start | bytes 1376264 | tf_op jit(solution)/shard_map/ppermute | solution.py:49
  32.3 21.1 %collective-permute-start.6 = (bf16[128,1792]{1,0:T(8,128)(2,1)S(1)}, bf16[128,1792]{1,0:T(8,128)(2,1)S(1)}, u32[]{:S(2)}, u32[]{:S(2)}) collective-permute-start(bf16[128,1792]{1,0:T(8,128)(2,1)S(1)} %collective-permute-done.1), channel_id=1, source_target_pairs={{0,2},{1,3},{2,4},{3,5},{4,6},{5,7},{6,0},{7,1},{8,10},{9,11},{10,... | collective-permute-start | bytes 1376264 | tf_op jit(solution)/shard_map/ppermute | solution.py:79
  41.5 14.2 %collective-permute-start.14 = (bf16[256,1024]{1,0:T(8,128)(2,1)S(1)}, bf16[256,1024]{1,0:T(8,128)(2,1)S(1)}, u32[]{:S(2)}, u32[]{:S(2)}) collective-permute-start(bf16[256,1024]{1,0:T(8,128)(2,1)S(1)} %pad_maximum_fusion.2), channel_id=1, source_target_pairs={{0,1},{1,0},{2,3},{3,2},{4,5},{5,4},{6,7},{7,6},{8,9},{9,8},{10,11... | collective-permute-start | bytes 1572872 | tf_op jit(solution)/shard_map/ppermute | solution.py:49
  43.7 11.1 %collective-permute-start.13 = (bf16[256,1792]{1,0:T(8,128)(2,1)S(1)}, bf16[256,1792]{1,0:T(8,128)(2,1)S(1)}, u32[]{:S(2)}, u32[]{:S(2)}) collective-permute-start(bf16[256,1792]{1,0:T(8,128)(2,1)S(1)} %bitcast.72), channel_id=1, source_target_pairs={{0,1},{1,0},{2,3},{3,2},{4,5},{5,4},{6,7},{7,6},{8,9},{9,8},{10,11... | collective-permute-start | bytes 2752520 | tf_op jit(solution)/shard_map/ppermute | solution.py:49
  49.9 13.1 %collective-permute-start.19 = (bf16[128,1792]{1,0:T(8,128)(2,1)S(1)}, bf16[128,1792]{1,0:T(8,128)(2,1)S(1)}, u32[]{:S(2)}, u32[]{:S(2)}) collective-permute-start(bf16[128,1792]{1,0:T(8,128)(2,1)S(1)} %collective-permute-done.7), channel_id=1, source_target_pairs={{0,2},{1,3},{2,4},{3,5},{4,6},{5,7},{6,0},{7,1},{8,10},{9,11},{10,... | collective-permute-start | bytes 1376264 | tf_op jit(solution)/shard_map/ppermute | solution.py:79
  53.4 12.6 %collective-permute-start.17 = (bf16[128,1792]{1,0:T(8,128)(2,1)S(1)}, bf16[128,1792]{1,0:T(8,128)(2,1)S(1)}, u32[]{:S(2)}, u32[]{:S(2)}) collective-permute-start(bf16[128,1792]{1,0:T(8,128)(2,1)S(1)} %collective-permute-done.7), channel_id=1, source_target_pairs={{0,1},{1,0},{2,3},{3,2},{4,5},{5,4},{6,7},{7,6},{8,9},{9,8},{10,11... | collective-permute-start | bytes 1376264 | tf_op jit(solution)/shard_map/ppermute | solution.py:49
  54.6 18.2 %collective-permute-start.10 = (bf16[128,1792]{1,0:T(8,128)(2,1)S(1)}, bf16[128,1792]{1,0:T(8,128)(2,1)S(1)}, u32[]{:S(2)}, u32[]{:S(2)}) collective-permute-start(bf16[128,1792]{1,0:T(8,128)(2,1)S(1)} %collective-permute-done.6), channel_id=1, source_target_pairs={{0,2},{1,3},{2,4},{3,5},{4,6},{5,7},{6,0},{7,1},{8,10},{9,11},{10,... | collective-permute-start | bytes 1376264 | tf_op jit(solution)/shard_map/ppermute | solution.py:79
  55.8 10.6 %collective-permute-start.18 = (bf16[128,1792]{1,0:T(8,128)(2,1)S(1)}, bf16[128,1792]{1,0:T(8,128)(2,1)S(1)}, u32[]{:S(2)}, u32[]{:S(2)}) collective-permute-start(bf16[128,1792]{1,0:T(8,128)(2,1)S(1)} %collective-permute-done.6), channel_id=1, source_target_pairs={{0,1},{1,0},{2,3},{3,2},{4,5},{5,4},{6,7},{7,6},{8,9},{9,8},{10,11... | collective-permute-start | bytes 1376264 | tf_op jit(solution)/shard_map/ppermute | solution.py:49
  79.7 14.3 %collective-permute-start.23 = (bf16[256,896]{1,0:T(8,128)(2,1)S(1)}, bf16[256,896]{1,0:T(8,128)(2,1)S(1)}, u32[]{:S(2)}, u32[]{:S(2)}) collective-permute-start(bf16[256,896]{1,0:T(8,128)(2,1)S(1)} %fusion.21), channel_id=1, source_target_pairs={{0,2},{1,3},{2,4},{3,5},{4,6},{5,7},{6,0},{7,1},{8,10},{9,11},{10,... | collective-permute-start | bytes 1376264 | tf_op jit(solution)/shard_map/ppermute | solution.py:79
  80.9 23.0 %collective-permute-start.26 = (bf16[256,896]{1,0:T(8,128)(2,1)S(1)}, bf16[256,896]{1,0:T(8,128)(2,1)S(1)}, u32[]{:S(2)}, u32[]{:S(2)}) collective-permute-start(bf16[256,896]{1,0:T(8,128)(2,1)S(1)} %fusion.22), channel_id=1, source_target_pairs={{0,2},{1,3},{2,4},{3,5},{4,6},{5,7},{6,0},{7,1},{8,10},{9,11},{10,... | collective-permute-start | bytes 1376264 | tf_op jit(solution)/shard_map/ppermute | solution.py:79
  81.0 25.6 %collective-permute-start.30 = (bf16[16384]{0:T(1024)(128)(2,1)S(1)}, bf16[16384]{0:T(1024)(128)(2,1)S(1)}, u32[]{:S(2)}, u32[]{:S(2)}) collective-permute-start(bf16[16384]{0:T(1024)(128)(2,1)S(1)} %add.363), channel_id=1, source_target_pairs={{0,128},{8,136},{16,144},{24,152},{32,160},{40,168},{48,176},{56,1... | collective-permute-start | bytes 98312 | tf_op jit(solution)/shard_map/ppermute | solution.py:49
  94.4 20.0 %collective-permute-start.25 = (bf16[256,896]{1,0:T(8,128)(2,1)S(1)}, bf16[256,896]{1,0:T(8,128)(2,1)S(1)}, u32[]{:S(2)}, u32[]{:S(2)}) collective-permute-start(bf16[256,896]{1,0:T(8,128)(2,1)S(1)} %fusion.23), channel_id=1, source_target_pairs={{0,2},{1,3},{2,4},{3,5},{4,6},{5,7},{6,0},{7,1},{8,10},{9,11},{10,... | collective-permute-start | bytes 1376264 | tf_op jit(solution)/shard_map/ppermute | solution.py:79
  104.2 20.0 %collective-permute-start.28 = (bf16[256,896]{1,0:T(8,128)(2,1)S(1)}, bf16[256,896]{1,0:T(8,128)(2,1)S(1)}, u32[]{:S(2)}, u32[]{:S(2)}) collective-permute-start(bf16[256,896]{1,0:T(8,128)(2,1)S(1)} %fusion.24), channel_id=1, source_target_pairs={{0,2},{1,3},{2,4},{3,5},{4,6},{5,7},{6,0},{7,1},{8,10},{9,11},{10,... | collective-permute-start | bytes 1376264 | tf_op jit(solution)/shard_map/ppermute | solution.py:79
  106.6 20.0 %collective-permute-start.31 = (bf16[16384]{0:T(1024)(128)(2,1)S(1)}, bf16[16384]{0:T(1024)(128)(2,1)S(1)}, u32[]{:S(2)}, u32[]{:S(2)}) collective-permute-start(bf16[16384]{0:T(1024)(128)(2,1)S(1)} %get-tuple-element.82), channel_id=1, source_target_pairs={{0,2},{1,3},{2,0},{3,1},{4,6},{5,7},{6,4},{7,5},{8,10},{9,11},{10,... | collective-permute-start | bytes 98312 | tf_op jit(solution)/shard_map/ppermute | solution.py:49
  114.8 35.1 %collective-permute-start.27 = (bf16[256,896]{1,0:T(8,128)(2,1)S(1)}, bf16[256,896]{1,0:T(8,128)(2,1)S(1)}, u32[]{:S(2)}, u32[]{:S(2)}) collective-permute-start(bf16[256,896]{1,0:T(8,128)(2,1)S(1)} %fusion.25), channel_id=1, source_target_pairs={{0,2},{1,3},{2,4},{3,5},{4,6},{5,7},{6,0},{7,1},{8,10},{9,11},{10,... | collective-permute-start | bytes 1376264 | tf_op jit(solution)/shard_map/ppermute | solution.py:79
  124.6 25.3 %collective-permute-start.29 = (bf16[256,896]{1,0:T(8,128)(2,1)S(1)}, bf16[256,896]{1,0:T(8,128)(2,1)S(1)}, u32[]{:S(2)}, u32[]{:S(2)}) collective-permute-start(bf16[256,896]{1,0:T(8,128)(2,1)S(1)} %fusion.26), channel_id=1, source_target_pairs={{0,2},{1,3},{2,4},{3,5},{4,6},{5,7},{6,0},{7,1},{8,10},{9,11},{10,... | collective-permute-start | bytes 1376264 | tf_op jit(solution)/shard_map/ppermute | solution.py:79
  126.6 21.6 %collective-permute-start.32 = (bf16[32768]{0:T(1024)(128)(2,1)S(1)}, bf16[32768]{0:T(1024)(128)(2,1)S(1)}, u32[]{:S(2)}, u32[]{:S(2)}) collective-permute-start(bf16[32768]{0:T(1024)(128)(2,1)S(1)} %pad_maximum_fusion.5), channel_id=1, source_target_pairs={{0,4},{1,5},{2,6},{3,7},{4,0},{5,1},{6,2},{7,3},{8,12},{9,13},{10,... | collective-permute-start | bytes 196616 | tf_op jit(solution)/shard_map/ppermute | solution.py:49
  (37 other events, 203.1 us)
